TPU v7x, 32 devices: a whole 2x2x4 slice. The times are simulated.
32 devices in a mesh: group: 2 (over y), dev: 16 (over z, x, core).
Axes of the slice: x: 2, y: 2, z: 4, core: 2. Of those that a mesh axis runs over, the one named last changes fastest.
Arguments:
- forces: float32 [3, 65536], P(None, ('group', 'dev')), may hold values from -4 to 4
- stencil_start: int32 [3, 65536], P(None, ('group', 'dev')), may hold values from 0 to 1023, as said below
- fraction: float32 [3, 65536], P(None, ('group', 'dev')), may hold values from 0 to 1
- tile_pairs: int32 [1536, 2], P(('group', 'dev')), may hold values from 0 to 15, as said below
- pair_count: int32 [32], P(('group', 'dev')), may hold values from 1 to 48, as said below
Outputs:
- velocity: float32 [3, 65536], P(None, ('group', 'dev'))
Inputs may be any that keep to these rules, and one draw needn't show every extreme that they name: `stencil_start`: along the first dimension, a point of block b = p // 2048 starts in planes b * 32 to (b + 1) * 32 - 1; along the others it lies in 0 to 127 and 0 to 127. `tile_pairs`: tile numbers are local to the device's block of 2048 points. `pair_count`: the live slots are the first ones of each device's list; some device has all 48 live.
All inputs are finite; a program needn't handle non-finite values.
Results may differ from a plain program's by a relative error of at most 0.0003.
Values sent between devices are 32-bit elements; how exact they have to be, the bound alone decides.
No kernel may reach another device: no remote copies, remote signals or barrier semaphores. Data moves between devices by JAX's collectives and lax.ppermute only.
A program may use at most 128 MiB of HBM per device.

v0:
```python
import jax
import jax.numpy as jnp
from jax import lax
from jax.sharding import PartitionSpec as P

NX = 1024
NY = 128
NZ = 128


TWO_PI = 6.283185307179586
EPS_SQ = 1.0
RANGE_SQ = 16.0
NEAR_SCALE = 0.25
FORM_Y = "cxky,yn->cxkn"
FORM_X = "cxky,xn->cnky"


def from_behind(x, axis, by):
    devices = lax.axis_size(axis)
    return lax.ppermute(x, axis, [(i, (i + by) % devices) for i in range(devices)])


def from_partner(x, axis, bit):
    return lax.ppermute(x, axis, [(i, i ^ 1 << bit) for i in range(lax.axis_size(axis))])


def spline_weights(fraction):
    square = fraction * fraction
    cube = square * fraction
    return [
        (1.0 - fraction) ** 3 / 6.0,
        (3.0 * cube - 6.0 * square + 4.0) / 6.0,
        (-3.0 * cube + 3.0 * square + 3.0 * fraction + 1.0) / 6.0,
        cube / 6.0,
    ]


def wave_numbers(index, length):
    signed_index = jnp.where(index > length // 2, index - length, index)
    return (signed_index.astype(jnp.float32) * (TWO_PI / length), index != length // 2)


def wrap_gap(gap, length):
    gap = jnp.where(gap > length // 2, gap - length, gap)
    return jnp.where(gap < -(length // 2), gap + length, gap)


def dft_tables(length):
    counter = jnp.arange(length, dtype=jnp.int32)
    product = counter[:, None] * counter[None, :] % length
    angle = product.astype(jnp.float32) * (TWO_PI / length)
    return (jnp.cos(angle), jnp.sin(angle))


def half_tables(length):
    counter = jnp.arange(length, dtype=jnp.int32)
    modes = jnp.arange(length // 2, dtype=jnp.int32)
    product = counter[:, None] * modes[None, :] % length
    angle = product.astype(jnp.float32) * (TWO_PI / length)
    return (jnp.cos(angle), jnp.sin(angle))


def apply_table(values, table, form):
    return jnp.einsum(form, values, table, precision=lax.Precision.HIGHEST)


def complex_along(real_part, imag_part, tables, form, sign):
    cosine, sine = tables
    real_cos = apply_table(real_part, cosine, form)
    real_sin = apply_table(real_part, sine, form)
    imag_cos = apply_table(imag_part, cosine, form)
    imag_sin = apply_table(imag_part, sine, form)
    return (real_cos - sign * imag_sin, imag_cos + sign * real_sin)


def twiddle(real_part, imag_part, angle):
    cosine = jnp.cos(angle)[None, :, None, None]
    sine = jnp.sin(angle)[None, :, None, None]
    return (real_part * cosine - imag_part * sine, imag_part * cosine + real_part * sine)


def stokes_modes(real_part, imag_part, index_x, index_y, index_z):
    wave_x, keep_x = wave_numbers(index_x, NX)
    wave_y, keep_y = wave_numbers(index_y, NY)
    wave_z, keep_z = wave_numbers(index_z, NZ)
    wave_x = wave_x[:, None, None]
    wave_z = wave_z[None, :, None]
    wave_y = wave_y[None, None, :]
    squared = wave_x * wave_x + wave_y * wave_y + wave_z * wave_z
    anchor = squared == 0
    keep = (
        keep_x[:, None, None]
        & keep_z[None, :, None]
        & keep_y[None, None, :]
        & jnp.logical_not(anchor)
    )
    inverse = jnp.where(keep, 1.0 / jnp.where(anchor, 1.0, squared), 0.0)
    waves = (wave_x, wave_y, wave_z)
    results = []
    for values in (real_part, imag_part):
        project = (wave_x * values[0] + wave_y * values[1] + wave_z * values[2]) * inverse
        results.append(
            jnp.stack(
                [
                    (values[component] - waves[component] * project) * inverse
                    for component in range(3)
                ]
            )
        )
    return (results[0], results[1])


def pair_terms(stencil_start, fraction, forces, pairs, count):
    tiles = stencil_start.shape[1] // 128
    slots = pairs.shape[0]
    start_tiles = stencil_start.reshape(3, tiles, 128)
    frac_tiles = fraction.reshape(3, tiles, 128)
    force_tiles = forces.reshape(3, tiles, 128)
    target = pairs[:, 0]
    source = pairs[:, 1]
    lengths = (NX, NY, NZ)
    deltas = []
    for component in range(3):
        gap = (
            start_tiles[component][target][:, :, None] - start_tiles[component][source][:, None, :]
        )
        if component > 0:
            gap = wrap_gap(gap, lengths[component])
        offset = (
            frac_tiles[component][target][:, :, None] - frac_tiles[component][source][:, None, :]
        )
        deltas.append(gap.astype(jnp.float32) + offset)
    distance = deltas[0] * deltas[0] + deltas[1] * deltas[1] + deltas[2] * deltas[2]
    softened = distance + EPS_SQ
    falloff = NEAR_SCALE * jnp.exp(-distance / RANGE_SQ) / (softened * jnp.sqrt(softened))
    diagonal = (distance + 2.0 * EPS_SQ) * falloff
    pulled = [force_tiles[component][source][:, None, :] for component in range(3)]
    along = deltas[0] * pulled[0] + deltas[1] * pulled[1] + deltas[2] * pulled[2]
    live = (jnp.arange(slots, dtype=jnp.int32) < count).astype(jnp.float32)[:, None]
    return jnp.stack(
        [
            jnp.sum(diagonal * pulled[component] + falloff * deltas[component] * along, axis=2)
            * live
            for component in range(3)
        ]
    )


def per_device(forces, stencil_start, fraction, tile_pairs, pair_count):
    groups = lax.axis_size("group")
    members = lax.axis_size("dev")
    planes = NX // (groups * members)
    points = forces.shape[1]
    tiles = points // 128
    side = lax.axis_index("group")
    member = lax.axis_index("dev")
    slab_first = (side * members + member) * planes
    weights = spline_weights(fraction)
    offset_x = stencil_start[0] - slab_first
    rows_x = jnp.arange(planes + 3, dtype=jnp.int32)[:, None]
    rows_y = jnp.arange(NY, dtype=jnp.int32)[:, None]
    rows_z = jnp.arange(NZ, dtype=jnp.int32)[:, None]
    weight_x = jnp.zeros((planes + 3, points), jnp.float32)
    weight_y = jnp.zeros((NY, points), jnp.float32)
    weight_z = jnp.zeros((NZ, points), jnp.float32)
    for stencil in range(4):
        weight_x = weight_x + jnp.where(
            rows_x == (offset_x + stencil)[None, :], weights[stencil][0][None, :], 0.0
        )
        weight_y = weight_y + jnp.where(
            rows_y == ((stencil_start[1] + stencil) % NY)[None, :],
            weights[stencil][1][None, :],
            0.0,
        )
        weight_z = weight_z + jnp.where(
            rows_z == ((stencil_start[2] + stencil) % NZ)[None, :],
            weights[stencil][2][None, :],
            0.0,
        )
    plane_weight = (weight_x[:, None, :] * weight_y[None, :, :]).reshape((planes + 3) * NY, points)
    spread = jnp.stack(
        [
            jnp.dot(
                plane_weight * forces[component][None, :],
                weight_z.T,
                precision=lax.Precision.HIGHEST,
            )
            for component in range(3)
        ]
    )
    spread = spread.reshape(3, planes + 3, NY, NZ)
    spilled = from_behind(spread[:, planes:], ("group", "dev"), 1)
    slab = spread[:, :planes].at[:, :3].add(spilled)
    forward_cos, forward_sin = half_tables(NZ)
    mode_weight = jnp.where(jnp.arange(NZ // 2, dtype=jnp.int32) == 0, 1.0, 2.0)
    back_cos = (forward_cos * mode_weight[None, :]).T
    back_sin = (forward_sin * mode_weight[None, :]).T
    tables_y = dft_tables(NY)
    real_part = apply_table(slab, forward_cos, "cxyz,zk->cxky")
    imag_part = -apply_table(slab, forward_sin, "cxyz,zk->cxky")
    real_part, imag_part = complex_along(real_part, imag_part, tables_y, FORM_Y, -1.0)
    real_part, imag_part = (
        lax.all_to_all(real_part, "dev", split_axis=3, concat_axis=1, tiled=True),
        lax.all_to_all(imag_part, "dev", split_axis=3, concat_axis=1, tiled=True),
    )
    rows_here = NY // members
    index_y = member * rows_here + jnp.arange(rows_here, dtype=jnp.int32)
    half = NX // groups
    sign_side = (1 - 2 * side).astype(jnp.float32)
    partner = from_partner((real_part, imag_part), "group", 0)
    real_part = real_part * sign_side + partner[0]
    imag_part = imag_part * sign_side + partner[1]
    counter = jnp.arange(half, dtype=jnp.int32).astype(jnp.float32)
    angle = side.astype(jnp.float32) * counter * (TWO_PI / NX)
    real_part, imag_part = twiddle(real_part, imag_part, -angle)
    tables_x = dft_tables(half)
    real_part, imag_part = complex_along(real_part, imag_part, tables_x, FORM_X, -1.0)
    index_x = 2 * jnp.arange(half, dtype=jnp.int32) + side
    index_z = jnp.arange(NZ // 2, dtype=jnp.int32)
    real_part, imag_part = stokes_modes(real_part, imag_part, index_x, index_y, index_z)
    real_part, imag_part = complex_along(real_part, imag_part, tables_x, FORM_X, 1.0)
    real_part, imag_part = twiddle(real_part, imag_part, angle)
    partner = from_partner((real_part, imag_part), "group", 0)
    real_part = partner[0] + sign_side * real_part
    imag_part = partner[1] + sign_side * imag_part
    real_part, imag_part = (
        lax.all_to_all(real_part, "dev", split_axis=1, concat_axis=3, tiled=True),
        lax.all_to_all(imag_part, "dev", split_axis=1, concat_axis=3, tiled=True),
    )
    real_part, imag_part = complex_along(real_part, imag_part, tables_y, FORM_Y, 1.0)
    field = apply_table(real_part, back_cos, "cxky,kz->cxyz") - apply_table(
        imag_part, back_sin, "cxky,kz->cxyz"
    )
    field = field / float(NX * NY * NZ)
    rim = from_behind(field[:, :3], ("group", "dev"), -1)
    extended = jnp.concatenate([field, rim], axis=1)
    far = jnp.stack(
        [
            jnp.sum(
                plane_weight
                * jnp.dot(
                    extended[component].reshape((planes + 3) * NY, NZ),
                    weight_z,
                    precision=lax.Precision.HIGHEST,
                ),
                axis=0,
            )
            for component in range(3)
        ]
    )
    terms = pair_terms(stencil_start, fraction, forces, tile_pairs, pair_count[0])
    onehot = (tile_pairs[:, 0][:, None] == jnp.arange(tiles, dtype=jnp.int32)[None, :]).astype(
        jnp.float32
    )
    near = jnp.einsum("st,csp->ctp", onehot, terms, precision=lax.Precision.HIGHEST).reshape(
        3, points
    )
    return far + near


def solution(mesh):
    in_specs = (
        P(None, ("group", "dev")),
        P(None, ("group", "dev")),
        P(None, ("group", "dev")),
        P(("group", "dev"), None),
        P(("group", "dev")),
    )
    out_specs = P(None, ("group", "dev"))
    return jax.shard_map(
        per_device, mesh=mesh, in_specs=in_specs, out_specs=out_specs, check_vma=False
    )
```

profile of v0, /device:TPU:0, one launch (start us, length us, event | category | flops | bytes accessed | tf_op | source)
XLA Modules:
  0.0 997.1 jit_solution(17462463994330059524)
XLA Ops:
  4.5 29.6 %fusion.62 = f32[1,35,128,128]{3,2,1,0:T(8,128)S(1)} fusion(f32[2048]{0:T(1024)S(1)} %bitcast.256, f32[128,2048]{1,0:T(8,128)S(1)} %select_add_fusion.1, f32[35,2048]{1,0:T(8,128)S(1)} %select_add_fusion.8, f32[128,2048,1]{1,0,2:T(8,128)S(1)} %fusion.301), kind=kOutput, calls=%fused_computation.111 | convolution fusion | flops 14111211520 | bytes 4685824 | tf_op jit(solution)/shard_map/dot_general | solution.py:184
  34.1 29.8 %fusion.61 = f32[1,35,128,128]{3,2,1,0:T(8,128)S(1)} fusion(f32[2048]{0:T(1024)S(1)} %bitcast.254, f32[128,2048]{1,0:T(8,128)S(1)} %select_add_fusion.1, f32[35,2048]{1,0:T(8,128)S(1)} %select_add_fusion.8, f32[128,2048,1]{1,0,2:T(8,128)S(1)} %fusion.299), kind=kOutput, calls=%fused_computation.110 | convolution fusion | flops 14111211520 | bytes 4685824 | tf_op jit(solution)/shard_map/dot_general | solution.py:184
  63.8 29.6 %fusion.60 = f32[1,35,128,128]{3,2,1,0:T(8,128)S(1)} fusion(f32[2048]{0:T(1024)S(1)} %bitcast.258, f32[128,2048]{1,0:T(8,128)S(1)} %select_add_fusion.1, f32[35,2048]{1,0:T(8,128)S(1)} %select_add_fusion.8, f32[128,2048,1]{1,0,2:T(8,128)S(1)} %fusion.297), kind=kOutput, calls=%fused_computation.109 | convolution fusion | flops 14111211520 | bytes 4685824 | tf_op jit(solution)/shard_map/dot_general | solution.py:184
  95.9 11.8 %collective-permute-done = f32[3,3,128,128]{3,2,1,0:T(8,128)S(1)} collective-permute-done((f32[3,3,128,128]{3,2,1,0:T(8,128)S(1)}, f32[3,3,128,128]{3,2,1,0:T(8,128)S(1)}, u32[]{:S(2)}, u32[]{:S(2)}) %collective-permute-start) | collective-permute-done | bytes 589856 | tf_op jit(solution)/shard_map/ppermute | solution.py:21
  171.4 38.7 %all-to-all-done.1 = f32[16,1,49152]{2,1,0:T(1,128)} async-done(((f32[16,1,49152]{2,1,0:T(1,128)}), f32[16,1,49152]{2,1,0:T(1,128)}, u32[]{:S(2)}, u32[]{:S(2)}) %all-to-all-start.1) | async-done | bytes 3145760 | tf_op jit(solution)/shard_map/all_to_all | solution.py:205
  210.1 15.7 %all-to-all-start = ((f32[16,1,49152]{2,1,0:T(1,128)}), f32[16,1,49152]{2,1,0:T(1,128)}, u32[]{:S(2)}, u32[]{:S(2)}) async-start(f32[16,1,49152]{2,1,0:T(1,128)} %reshape.780), calls=%async_computation | async-start | bytes 6291456 | tf_op jit(solution)/shard_map/all_to_all | solution.py:204
  240.8 11.4 %copy.47 = f32[3,16,32,64,8]{3,4,2,1,0:T(8,128)} copy(f32[3,16,32,64,8]{3,2,0,4,1:T(8,128)} %bitcast.233) | data formatting | bytes 6291456 | tf_op jit(solution)/shard_map/all_to_all | solution.py:205
  257.0 28.1 %all-to-all-done = f32[16,1,49152]{2,1,0:T(1,128)} async-done(((f32[16,1,49152]{2,1,0:T(1,128)}), f32[16,1,49152]{2,1,0:T(1,128)}, u32[]{:S(2)}, u32[]{:S(2)}) %all-to-all-start) | async-done | bytes 3145760 | tf_op jit(solution)/shard_map/all_to_all | solution.py:204
  285.2 11.7 %reduce.2 = f32[16,49152]{1,0:T(8,128)} reduce(f32[16,1,49152]{2,1,0:T(1,128)} %all-to-all-done, f32[]{:T(128)} %broadcast.1085), dimensions={1}, to_apply=%all_to_all.52.reduce_sub_computation | reduce | bytes 6291460 | tf_op jit(solution)/shard_map/all_to_all | solution.py:204
  322.6 68.9 %collective-permute-done.1 = f32[3,512,64,8]{1,2,3,0:T(8,128)} collective-permute-done((f32[3,512,64,8]{1,2,3,0:T(8,128)}, f32[3,512,64,8]{1,2,3,0:T(8,128)}, u32[]{:S(2)}, u32[]{:S(2)}) %collective-permute-start.1) | collective-permute-done | bytes 3145760 | tf_op jit(solution)/shard_map/ppermute | solution.py:25
  391.5 67.4 %collective-permute-done.2 = f32[3,512,64,8]{1,2,3,0:T(8,128)} collective-permute-done((f32[3,512,64,8]{1,2,3,0:T(8,128)S(1)}, f32[3,512,64,8]{1,2,3,0:T(8,128)}, u32[]{:S(2)}, u32[]{:S(2)}) %collective-permute-start.2) | collective-permute-done | bytes 3145760 | tf_op jit(solution)/shard_map/ppermute | solution.py:25
  464.2 11.5 %fusion.73 = f32[512,3,64,8]{0,2,3,1:T(8,128)S(1)} fusion(f32[3,512,64,8]{1,2,3,0:T(8,128)S(1)} %get-tuple-element.26), kind=kOutput, calls=%fused_computation.128 | convolution fusion | flops 4835508224 | bytes 6291456 | tf_op jit(solution)/shard_map/cxky,xn->cnky/dot_general | solution.py:65
  487.1 11.7 %subtract_bitcast_fusion.1 = f32[3,512,64,8]{1,2,3,0:T(8,128)S(1)} fusion(f32[512,3,64,8]{0,2,3,1:T(8,128)S(1)} %fusion.73, f32[3,512,64,8]{1,2,3,0:T(8,128)S(1)} %get-tuple-element.27), kind=kOutput, calls=%fused_computation.91 | convolution fusion | flops 4837081088 | bytes 9437184 | tf_op jit(solution)/shard_map/cxky,xn->cnky/dot_general | solution.py:65
  498.8 11.5 %add_bitcast_fusion.1 = f32[3,512,64,8]{1,2,3,0:T(8,128)S(1)} fusion(f32[512,3,64,8]{0,2,3,1:T(8,128)S(1)} %fusion.71, f32[3,512,64,8]{1,2,3,0:T(8,128)S(1)} %get-tuple-element.26), kind=kOutput, calls=%fused_computation.90 | convolution fusion | flops 4837081088 | bytes 9437184 | tf_op jit(solution)/shard_map/cxky,xn->cnky/dot_general | solution.py:65
  552.4 68.4 %collective-permute-done.3 = f32[3,512,64,8]{1,2,3,0:T(8,128)S(1)} collective-permute-done((f32[3,512,64,8]{1,2,3,0:T(8,128)S(1)}, f32[3,512,64,8]{1,2,3,0:T(8,128)S(1)}, u32[]{:S(2)}, u32[]{:S(2)}) %collective-permute-start.3) | collective-permute-done | bytes 3145760 | tf_op jit(solution)/shard_map/ppermute | solution.py:25
  637.7 14.6 %all-to-all-start.2 = ((f32[16,1,49152]{2,1,0:T(1,128)}), f32[16,1,49152]{2,1,0:T(1,128)}, u32[]{:S(2)}, u32[]{:S(2)}) async-start(f32[16,1,49152]{2,1,0:T(1,128)} %reshape.786), calls=%async_computation.2 | async-start | bytes 6291456 | tf_op jit(solution)/shard_map/all_to_all | solution.py:228
  653.9 68.8 %collective-permute-done.4 = f32[3,512,64,8]{1,2,3,0:T(8,128)S(1)} collective-permute-done((f32[3,512,64,8]{1,2,3,0:T(8,128)S(1)}, f32[3,512,64,8]{1,2,3,0:T(8,128)S(1)}, u32[]{:S(2)}, u32[]{:S(2)}) %collective-permute-start.4) | collective-permute-done | bytes 3145760 | tf_op jit(solution)/shard_map/ppermute | solution.py:25
  762.0 12.4 %broadcast_multiply_fusion = f32[35,128,2048]{2,1,0:T(8,128)} fusion(f32[128,2048]{1,0:T(8,128)S(1)} %copy-done.9, f32[35,2048]{1,0:T(8,128)S(1)} %select_add_fusion.8), kind=kLoop, calls=%fused_computation.33 | loop fusion | flops 9175040 | bytes 38035456 | tf_op jit(solution)/shard_map/mul | solution.py:181
  788.6 13.9 %fusion.19 = f32[3,32,64,128]{3,2,1,0:T(8,128)} fusion(f32[3,32,64,16,8]{2,4,0,1,3:T(8,128)} %bitcast.227), kind=kOutput, calls=%fused_computation.50 | convolution fusion | flops 1208188928 | bytes 6291456 | tf_op jit(solution)/shard_map/cxky,yn->cxkn/dot_general | solution.py:65
  812.6 11.8 %reduce.4 = f32[16,49152]{1,0:T(8,128)} reduce(f32[16,1,49152]{2,1,0:T(1,128)} %all-to-all-done.3, f32[]{:T(128)} %broadcast.1085), dimensions={1}, to_apply=%all_to_all.64.reduce_sub_computation | reduce | bytes 6291460 | tf_op jit(solution)/shard_map/all_to_all | solution.py:229
  830.0 12.6 %fusion.15 = f32[3,32,64,128]{3,2,1,0:T(8,128)S(1)} fusion(f32[3,32,64,16,8]{2,4,0,1,3:T(8,128)} %bitcast.229), kind=kOutput, calls=%fused_computation.46 | convolution fusion | flops 1208188928 | bytes 6291456 | tf_op jit(solution)/shard_map/cxky,yn->cxkn/dot_general | solution.py:65
  894.0 34.0 %fusion.4 = f32[2048]{0:T(1024)S(1)} fusion(f32[35,128,2048]{2,1,0:T(8,128)} %broadcast_multiply_fusion, f32[4480,128]{1,0:T(8,128)S(1)} %bitcast.253, f32[2048]{0:T(1024)S(1)} %bitcast.305, s32[2048]{0:T(1024)S(1)} %bitcast.269, f32[2048]{0:T(1024)S(1)} %bitcast.299, s32[2048]{0:T(1024)S(1)} %bitcast.281, f32[2048]{0:T(1024)S(1)} %bitcast.293, ...), kind=kOutput, calls=%fused_computation.25 | convolution fusion | flops 14114093056 | bytes 39067648 | tf_op jit(solution)/shard_map/dot_general | solution.py:242
  928.0 34.2 %fusion.5 = f32[2048]{0:T(1024)S(1)} fusion(f32[35,128,2048]{2,1,0:T(8,128)} %broadcast_multiply_fusion, f32[4480,128]{1,0:T(8,128)S(1)} %bitcast.252, f32[2048]{0:T(1024)S(1)} %bitcast.306, s32[2048]{0:T(1024)S(1)} %bitcast.270, f32[2048]{0:T(1024)S(1)} %bitcast.300, s32[2048]{0:T(1024)S(1)} %bitcast.282, f32[2048]{0:T(1024)S(1)} %bitcast.294, ...), kind=kOutput, calls=%fused_computation.26 | convolution fusion | flops 14114093056 | bytes 39067648 | tf_op jit(solution)/shard_map/dot_general | solution.py:242
  962.2 34.0 %fusion.3 = f32[2048]{0:T(1024)S(1)} fusion(f32[35,128,2048]{2,1,0:T(8,128)} %broadcast_multiply_fusion, f32[4480,128]{1,0:T(8,128)S(1)} %bitcast.251, f32[2048]{0:T(1024)S(1)} %bitcast.307, s32[2048]{0:T(1024)S(1)} %bitcast.271, f32[2048]{0:T(1024)S(1)} %bitcast.301, s32[2048]{0:T(1024)S(1)} %bitcast.283, f32[2048]{0:T(1024)S(1)} %bitcast.295, ...), kind=kOutput, calls=%fused_computation.24 | convolution fusion | flops 14114093056 | bytes 39067648 | tf_op jit(solution)/shard_map/dot_general | solution.py:242
  (186 shorter events, 313.3 us)
Async XLA Ops:
  4.4 59.4 %copy-start.8 = (f32[128,2048]{1,0:T(8,128)}, f32[128,2048]{1,0:T(8,128)S(1)}, u32[]{:S(2)}) copy-start(f32[128,2048]{1,0:T(8,128)S(1)} %select_add_fusion.1) | copy-start | bytes 3145732
  93.5 14.2 %collective-permute-start = (f32[3,3,128,128]{3,2,1,0:T(8,128)S(1)}, f32[3,3,128,128]{3,2,1,0:T(8,128)S(1)}, u32[]{:S(2)}, u32[]{:S(2)}) collective-permute-start(f32[3,3,128,128]{3,2,1,0:T(8,128)S(1)} %pad_maximum_fusion.12), channel_id=1, source_target_pairs={{0,1},{1,2},{2,3},{3,4},{4,5},{5,6},{6,7},{7,8},{8,9},{9,10},{10,1... | collective-permute-start | bytes 1769480 | tf_op jit(solution)/shard_map/ppermute | solution.py:21
  146.1 64.0 %all-to-all-start.1 = ((f32[16,1,49152]{2,1,0:T(1,128)}), f32[16,1,49152]{2,1,0:T(1,128)}, u32[]{:S(2)}, u32[]{:S(2)}) async-start(f32[16,1,49152]{2,1,0:T(1,128)} %reshape.782), calls=%async_computation.1 | async-start | bytes 6291456 | tf_op jit(solution)/shard_map/all_to_all | solution.py:205
  210.1 75.1 %all-to-all-start = ((f32[16,1,49152]{2,1,0:T(1,128)}), f32[16,1,49152]{2,1,0:T(1,128)}, u32[]{:S(2)}, u32[]{:S(2)}) async-start(f32[16,1,49152]{2,1,0:T(1,128)} %reshape.780), calls=%async_computation | async-start | bytes 6291456 | tf_op jit(solution)/shard_map/all_to_all | solution.py:204
  320.2 71.3 %collective-permute-start.1 = (f32[3,512,64,8]{1,2,3,0:T(8,128)}, f32[3,512,64,8]{1,2,3,0:T(8,128)}, u32[]{:S(2)}, u32[]{:S(2)}) collective-permute-start(f32[3,512,64,8]{1,2,3,0:T(8,128)} %copy.43), channel_id=1, source_target_pairs={{0,16},{16,0},{1,17},{17,1},{2,18},{18,2},{3,19},{19,3},{4,20},{20... | collective-permute-start | bytes 9437192 | tf_op jit(solution)/shard_map/ppermute | solution.py:25
  322.1 136.8 %collective-permute-start.2 = (f32[3,512,64,8]{1,2,3,0:T(8,128)S(1)}, f32[3,512,64,8]{1,2,3,0:T(8,128)}, u32[]{:S(2)}, u32[]{:S(2)}) collective-permute-start(f32[3,512,64,8]{1,2,3,0:T(8,128)S(1)} %copy.48), channel_id=1, source_target_pairs={{0,16},{16,0},{1,17},{17,1},{2,18},{18,2},{3,19},{19,3},{4,20},{20... | collective-permute-start | bytes 9437192 | tf_op jit(solution)/shard_map/ppermute | solution.py:25
  550.6 70.2 %collective-permute-start.3 = (f32[3,512,64,8]{1,2,3,0:T(8,128)S(1)}, f32[3,512,64,8]{1,2,3,0:T(8,128)S(1)}, u32[]{:S(2)}, u32[]{:S(2)}) collective-permute-start(f32[3,512,64,8]{1,2,3,0:T(8,128)S(1)} %get-tuple-element.31), channel_id=1, source_target_pairs={{0,16},{16,0},{1,17},{17,1},{2,18},{18,2},{3,19},{19,3},{4,20},{20... | collective-permute-start | bytes 9437192 | tf_op jit(solution)/shard_map/ppermute | solution.py:25
  637.7 101.9 %all-to-all-start.2 = ((f32[16,1,49152]{2,1,0:T(1,128)}), f32[16,1,49152]{2,1,0:T(1,128)}, u32[]{:S(2)}, u32[]{:S(2)}) async-start(f32[16,1,49152]{2,1,0:T(1,128)} %reshape.786), calls=%async_computation.2 | async-start | bytes 6291456 | tf_op jit(solution)/shard_map/all_to_all | solution.py:228
  652.3 70.4 %collective-permute-start.4 = (f32[3,512,64,8]{1,2,3,0:T(8,128)S(1)}, f32[3,512,64,8]{1,2,3,0:T(8,128)S(1)}, u32[]{:S(2)}, u32[]{:S(2)}) collective-permute-start(f32[3,512,64,8]{1,2,3,0:T(8,128)S(1)} %get-tuple-element.32), channel_id=1, source_target_pairs={{0,16},{16,0},{1,17},{17,1},{2,18},{18,2},{3,19},{19,3},{4,20},{20... | collective-permute-start | bytes 9437192 | tf_op jit(solution)/shard_map/ppermute | solution.py:25
  739.6 73.0 %all-to-all-start.3 = ((f32[16,1,49152]{2,1,0:T(1,128)}), f32[16,1,49152]{2,1,0:T(1,128)}, u32[]{:S(2)}, u32[]{:S(2)}) async-start(f32[16,1,49152]{2,1,0:T(1,128)} %reshape.784), calls=%async_computation.3 | async-start | bytes 6291456 | tf_op jit(solution)/shard_map/all_to_all | solution.py:229
  863.5 17.9 %copy-start.27 = (f32[48,128]{1,0:T(8,128)S(1)}, f32[48,128]{1,0:T(8,128)}, u32[]{:S(2)}) copy-start(f32[48,128]{1,0:T(8,128)} %gather_fusion.7) | copy-start | bytes 73732
  863.5 17.9 %copy-start.28 = (f32[48,128]{1,0:T(8,128)S(1)}, f32[48,128]{1,0:T(8,128)}, u32[]{:S(2)}) copy-start(f32[48,128]{1,0:T(8,128)} %gather_fusion.6) | copy-start | bytes 73732
  863.5 17.9 %copy-start.29 = (f32[48,128]{1,0:T(8,128)S(1)}, f32[48,128]{1,0:T(8,128)}, u32[]{:S(2)}) copy-start(f32[48,128]{1,0:T(8,128)} %gather_fusion.11) | copy-start | bytes 73732
  863.5 17.9 %copy-start.30 = (f32[48,128]{1,0:T(8,128)S(1)}, f32[48,128]{1,0:T(8,128)}, u32[]{:S(2)}) copy-start(f32[48,128]{1,0:T(8,128)} %gather_fusion.10) | copy-start | bytes 73732
  863.5 17.9 %copy-start.31 = (s32[48,128]{1,0:T(8,128)S(1)}, s32[48,128]{1,0:T(8,128)}, u32[]{:S(2)}) copy-start(s32[48,128]{1,0:T(8,128)} %gather_fusion.1) | copy-start | bytes 73732
  863.5 17.9 %copy-start.32 = (s32[48,128]{1,0:T(8,128)S(1)}, s32[48,128]{1,0:T(8,128)}, u32[]{:S(2)}) copy-start(s32[48,128]{1,0:T(8,128)} %gather_fusion) | copy-start | bytes 73732
  863.5 17.9 %copy-start.33 = (s32[48,128]{1,0:T(8,128)S(1)}, s32[48,128]{1,0:T(8,128)}, u32[]{:S(2)}) copy-start(s32[48,128]{1,0:T(8,128)} %gather_fusion.9) | copy-start | bytes 73732
  863.6 17.9 %copy-start.34 = (s32[48,128]{1,0:T(8,128)S(1)}, s32[48,128]{1,0:T(8,128)}, u32[]{:S(2)}) copy-start(s32[48,128]{1,0:T(8,128)} %gather_fusion.8) | copy-start | bytes 73732
  863.6 17.9 %copy-start.35 = (s32[48,128]{1,0:T(8,128)S(1)}, s32[48,128]{1,0:T(8,128)}, u32[]{:S(2)}) copy-start(s32[48,128]{1,0:T(8,128)} %gather_fusion.4) | copy-start | bytes 73732
  863.6 17.9 %copy-start.36 = (s32[48,128]{1,0:T(8,128)S(1)}, s32[48,128]{1,0:T(8,128)}, u32[]{:S(2)}) copy-start(s32[48,128]{1,0:T(8,128)} %gather_fusion.5) | copy-start | bytes 73732
  863.6 17.9 %copy-start.37 = (f32[48,128]{1,0:T(8,128)S(1)}, f32[48,128]{1,0:T(8,128)}, u32[]{:S(2)}) copy-start(f32[48,128]{1,0:T(8,128)} %gather_fusion.14) | copy-start | bytes 73732
  863.6 17.9 %copy-start.38 = (f32[48,128]{1,0:T(8,128)S(1)}, f32[48,128]{1,0:T(8,128)}, u32[]{:S(2)}) copy-start(f32[48,128]{1,0:T(8,128)} %gather_fusion.12) | copy-start | bytes 73732
  863.6 17.9 %copy-start.39 = (f32[48,128]{1,0:T(8,128)S(1)}, f32[48,128]{1,0:T(8,128)}, u32[]{:S(2)}) copy-start(f32[48,128]{1,0:T(8,128)} %gather_fusion.13) | copy-start | bytes 73732
  874.1 19.0 %collective-permute-start.5 = (f32[3,3,128,128]{3,2,1,0:T(8,128)S(1)}, f32[3,3,128,128]{3,2,1,0:T(8,128)S(1)}, u32[]{:S(2)}, u32[]{:S(2)}) collective-permute-start(f32[3,3,128,128]{3,2,1,0:T(8,128)S(1)} %slice.266), channel_id=1, source_target_pairs={{0,31},{1,0},{2,1},{3,2},{4,3},{5,4},{6,5},{7,6},{8,7},{9,8},{10,9... | collective-permute-start | bytes 1769480 | tf_op jit(solution)/shard_map/ppermute | solution.py:21
  (28 other events, 141.0 us)
where the time goes:
time: 1010 us; the launch traced here: 997 us
  matrix products  371 us (37%)
  waiting for transfers between devices  352 us (35%)
  local copies, waits for them, and re-layouts  131 us (13%)
  other arithmetic  86.3 us (9%)
  starting transfers between devices  54.3 us (5%)
    ppermute x4, waiting for transfers between devices, from_partner(): lax.ppermute(x, axis, [(i, i ^ 1 << bit) for i in range(lax.axis_size(axi...  273 us
    dot_general x20, matrix products, apply_table(): return jnp.einsum(form, values, table, precision=lax.Precision.HIGHEST)  180 us
    dot_general x3, matrix products, per_device(): jnp.dot(extended[component].reshape((planes + 3) * NY, NZ), weight_z, pre...  102 us
    dot_general x3, matrix products, per_device(): jnp.dot(plane_weight * forces[component][None, :], weight_z.T, precision=...  88.9 us
    unnamed x92, local copies, waits for them, and re-layouts  54.2 us
    all_to_all x1, waiting for transfers between devices, per_device(): lax.all_to_all(imag_part, 'dev', split_axis=3, concat_axis=1, tiled=True)  38.7 us
    all_to_all x1, waiting for transfers between devices, per_device(): lax.all_to_all(real_part, 'dev', split_axis=3, concat_axis=1, tiled=True)  28.1 us
  transfers between devices with their start and end apart: 10, of which 7 were waited for; matrix products, arithmetic and copies ran while one was open for 15% of the time, Pallas kernels for 0%

commit v1 on v0

v1 whole, which is shorter than its diff:
```python
import functools

import jax
import jax.numpy as jnp
import ml_dtypes
import numpy as np
from jax import lax
from jax.experimental import pallas as pl
from jax.experimental.pallas import tpu as pltpu
from jax.sharding import PartitionSpec as P

NX = 1024
NY = 128
NZ = 128

TWO_PI = 6.283185307179586
EPS_SQ = 1.0
RANGE_SQ = 16.0
NEAR_SCALE = 0.25

LANES = 128
KZ = 16
KY = 8
COLS = 4 * KY * KZ
CHUNK = 512
BF16 = jnp.bfloat16
F32 = jnp.float32


def wrap_gap(gap, length):
    gap = jnp.where(gap > length // 2, gap - length, gap)
    return jnp.where(gap < -(length // 2), gap + length, gap)


def pair_terms(stencil_start, fraction, forces, pairs, count):
    tiles = stencil_start.shape[1] // 128
    slots = pairs.shape[0]
    start_tiles = stencil_start.reshape(3, tiles, 128)
    frac_tiles = fraction.reshape(3, tiles, 128)
    force_tiles = forces.reshape(3, tiles, 128)
    target = pairs[:, 0]
    source = pairs[:, 1]
    lengths = (NX, NY, NZ)
    deltas = []
    for component in range(3):
        gap = (
            start_tiles[component][target][:, :, None] - start_tiles[component][source][:, None, :]
        )
        if component > 0:
            gap = wrap_gap(gap, lengths[component])
        offset = (
            frac_tiles[component][target][:, :, None] - frac_tiles[component][source][:, None, :]
        )
        deltas.append(gap.astype(jnp.float32) + offset)
    distance = deltas[0] * deltas[0] + deltas[1] * deltas[1] + deltas[2] * deltas[2]
    softened = distance + EPS_SQ
    falloff = NEAR_SCALE * jnp.exp(-distance / RANGE_SQ) / (softened * jnp.sqrt(softened))
    diagonal = (distance + 2.0 * EPS_SQ) * falloff
    pulled = [force_tiles[component][source][:, None, :] for component in range(3)]
    along = deltas[0] * pulled[0] + deltas[1] * pulled[1] + deltas[2] * pulled[2]
    live = (jnp.arange(slots, dtype=jnp.int32) < count).astype(jnp.float32)[:, None]
    return jnp.stack(
        [
            jnp.sum(diagonal * pulled[component] + falloff * deltas[component] * along, axis=2)
            * live
            for component in range(3)
        ]
    )


def split(value):
    high = value.astype(BF16)
    low = (value - high.astype(F32)).astype(BF16)
    return high, low


def spline_weights(fraction):
    square = fraction * fraction
    cube = square * fraction
    rest = 1.0 - fraction
    return [
        rest * rest * rest * (1.0 / 6.0),
        (3.0 * cube - 6.0 * square + 4.0) * (1.0 / 6.0),
        (-3.0 * cube + 3.0 * square + 3.0 * fraction + 1.0) * (1.0 / 6.0),
        cube * (1.0 / 6.0),
    ]


def cos_sin_turns(turns):
    part = turns - jnp.floor(turns + 0.5)
    half = part * (0.5 * TWO_PI)
    square = half * half
    sine = half * (
        1.0
        + square
        * (
            -1.0 / 6.0
            + square
            * (1.0 / 120.0 + square * (-1.0 / 5040.0 + square * (1.0 / 362880.0 + square * (-1.0 / 39916800.0))))
        )
    )
    cosine = 1.0 + square * (
        -0.5
        + square
        * (
            1.0 / 24.0
            + square
            * (-1.0 / 720.0 + square * (1.0 / 40320.0 + square * (-1.0 / 3628800.0 + square * (1.0 / 479001600.0))))
        )
    )
    return 1.0 - 2.0 * sine * sine, 2.0 * sine * cosine


def widen(table, width):
    return jnp.concatenate([table] * (width // LANES), axis=1)


def mode_rows(start, weights, modes, length):
    width = start.shape[1]
    cosine, sine = cos_sin_turns(widen(modes[0], width) * start * (1.0 / length))
    sum_cos = weights[0] + weights[1] * widen(modes[1], width)
    sum_sin = weights[1] * widen(modes[2], width)
    sum_cos = sum_cos + weights[2] * widen(modes[3], width) + weights[3] * widen(modes[5], width)
    sum_sin = sum_sin + weights[2] * widen(modes[4], width) + weights[3] * widen(modes[6], width)
    return cosine * sum_cos - sine * sum_sin, sine * sum_cos + cosine * sum_sin


def column_values(points, modes_y, modes_z):
    weights = spline_weights(points[6:9])
    rows_y = mode_rows(points[4:5], [w[1:2] for w in weights], modes_y, NY)
    rows_z = mode_rows(points[5:6], [w[2:3] for w in weights], modes_z, NZ)
    values = []
    for ty in range(2):
        for tz in range(2):
            for iy in range(KY):
                values.append(rows_y[ty][iy : iy + 1] * rows_z[tz])
    return values, [w[0:1] for w in weights]


def plane_rows(start, weights, rows):
    iota = lax.broadcasted_iota(jnp.int32, (rows, start.shape[1]), 0).astype(F32)
    away = iota - start
    result = jnp.where(away == 0.0, weights[0], 0.0)
    for stencil in range(1, 4):
        result = jnp.where(away == float(stencil), weights[stencil], result)
    return result


def chunk_of(points_ref, index):
    per_block = points_ref.shape[2] // CHUNK
    at = pl.ds(pl.multiple_of(lax.rem(index, per_block) * CHUNK, CHUNK), CHUNK)
    return points_ref[lax.div(index, per_block), :, at]


def spread_kernel(planes, rows, points_ref, modes_y_ref, modes_z_ref, out_ref, acc):
    step = pl.program_id(0)
    chunk = CHUNK
    count = points_ref.shape[0] * points_ref.shape[2] // chunk

    @pl.when(step == 0)
    def _():
        out_ref[...] = jnp.zeros_like(out_ref)

    modes_y = [modes_y_ref[i] for i in range(7)]
    modes_z = [modes_z_ref[i] for i in range(7)]

    def one(index):
        points = chunk_of(points_ref, index)
        values, weights_x = column_values(points, modes_y, modes_z)
        weight = plane_rows(points[3:4], weights_x, rows)
        stack = jnp.concatenate([weight * points[c : c + 1] for c in range(3)], axis=0)
        if 3 * rows < LANES:
            stack = jnp.concatenate([stack, jnp.zeros((LANES - 3 * rows, chunk), F32)], axis=0)
        high, low = split(stack)
        both = jnp.concatenate([high, low], axis=0)
        highs, lows = [], []
        for value in values:
            h, l = split(value)
            highs.append(h)
            lows.append(l)
        left = jnp.concatenate([jnp.concatenate(highs, axis=0), jnp.concatenate(lows, axis=0)], axis=1)
        right = jnp.concatenate([both, both], axis=1)
        return lax.dot_general(
            left, right, (((1,), (1,)), ((), ())), preferred_element_type=F32
        )

    acc[...] = jnp.zeros_like(acc)

    @pl.loop(0, count)
    def _(index):
        acc[...] += one(index)

    total = (acc[:, :LANES] + acc[:, LANES:]).T
    first = pl.multiple_of(step * planes, 8)
    for c in range(3):
        out_ref[c, pl.ds(first, rows)] += total[c * rows : (c + 1) * rows]

    @pl.when(step == pl.num_programs(0) - 1)
    def _():
        extra = out_ref.shape[1] - NX
        for c in range(3):
            out_ref[c, 0:extra] += out_ref[c, NX : NX + extra]


def spread(points, modes_y, modes_z, planes, rows, joined):
    blocks, _, count = points.shape
    extra = rows - planes
    return pl.pallas_call(
        functools.partial(spread_kernel, planes, rows),
        grid=(blocks // joined,),
        in_specs=[
            pl.BlockSpec((joined, 9, count), lambda i: (i, 0, 0)),
            pl.BlockSpec(modes_y.shape, lambda i: (0, 0, 0)),
            pl.BlockSpec(modes_z.shape, lambda i: (0, 0, 0)),
        ],
        out_specs=pl.BlockSpec((3, NX + extra, COLS), lambda i: (0, 0, 0)),
        out_shape=jax.ShapeDtypeStruct((3, NX + extra, COLS), F32),
        scratch_shapes=[
            pltpu.VMEM((COLS, 2 * LANES), F32),
        ],
        compiler_params=pltpu.CompilerParams(vmem_limit_bytes=56 * 2**20),
        name="spread",
    )(points, modes_y, modes_z)


def solve_kernel(extra, spread_ref, forward_ref, back_ref, waves_ref, scale_ref, out_ref, modes, stacked):
    half = NX // 2
    quarter = NX // 4
    lanes = COLS // 4

    def fill(value):
        high, low = split(value)
        stacked[0:half] = high
        stacked[half : 2 * half] = high
        stacked[2 * half : 3 * half] = low

    for parity in range(2):

        @pl.loop(0, 3)
        def _(c):
            first = spread_ref[c, 0:half]
            second = spread_ref[c, half:NX]
            fill(first + second if parity == 0 else first - second)
            modes[parity, c] = jnp.dot(forward_ref[parity], stacked[...], preferred_element_type=F32)

    wave_y = waves_ref[0:1]
    wave_z = waves_ref[1:2]
    mult = waves_ref[2:3]
    flat = wave_y * wave_y + wave_z * wave_z
    group = 8

    for parity in range(2):

        @pl.loop(0, quarter // group)
        def _(index):
            row = pl.multiple_of(index * group, group)
            number = lax.broadcasted_iota(jnp.int32, (group, lanes), 0) + row
            number = (2 * number + parity).astype(F32)
            wave_x = number * (TWO_PI / NX)
            squared = wave_x * wave_x + flat
            anchor = squared == 0.0
            inverse = jnp.where(anchor, 0.0, 1.0 / jnp.where(anchor, 1.0, squared))
            factor = inverse * mult * jnp.where(number == 0.0, 1.0, 2.0)
            waves = (wave_x, wave_y, wave_z)
            values = {}
            for c in range(3):
                for tx in range(2):
                    for tyz in range(4):
                        values[c, tx, tyz // 2, tyz % 2] = modes[
                            parity,
                            c,
                            pl.ds(pl.multiple_of(tx * quarter + row, group), group),
                            tyz * lanes : (tyz + 1) * lanes,
                        ]

            def flip(state, axis):
                return tuple(1 - t if i == axis else t for i, t in enumerate(state))

            states = [(a, b, d) for a in range(2) for b in range(2) for d in range(2)]
            divergence = {}
            for state in states:
                total = None
                for axis in range(3):
                    term = waves[axis] * values[(axis,) + flip(state, axis)]
                    if state[axis]:
                        term = -term
                    total = term if total is None else total + term
                divergence[state] = total * inverse
            for state in states:
                for axis in range(3):
                    term = waves[axis] * divergence[flip(state, axis)]
                    value = values[(axis,) + state]
                    value = value - term if state[axis] else value + term
                    tyz = 2 * state[1] + state[2]
                    modes[
                        parity,
                        axis,
                        pl.ds(pl.multiple_of(state[0] * quarter + row, group), group),
                        tyz * lanes : (tyz + 1) * lanes,
                    ] = value * factor

    @pl.loop(0, 3)
    def _(c):
        fill(modes[0, c])
        even = jnp.dot(back_ref[0], stacked[...], preferred_element_type=F32)
        out_ref[c, 0:half] = even
        fill(modes[1, c])
        odd = jnp.dot(back_ref[1], stacked[...], preferred_element_type=F32)
        even = out_ref[c, 0:half]
        out_ref[c, 0:half] = even + odd
        out_ref[c, half:NX] = even - odd
        out_ref[c, NX : NX + extra] = out_ref[c, 0:extra]


def solve(spectrum, waves, forward, back):
    extra = spectrum.shape[1] - NX
    full = pl.BlockSpec(memory_space=pltpu.VMEM)
    return pl.pallas_call(
        functools.partial(solve_kernel, extra),
        in_specs=[full] * 5,
        out_specs=full,
        out_shape=jax.ShapeDtypeStruct(spectrum.shape, F32),
        scratch_shapes=[
            pltpu.VMEM((2, 3, NX // 2, COLS), F32),
            pltpu.VMEM((3 * NX // 2, COLS), BF16),
        ],
        compiler_params=pltpu.CompilerParams(vmem_limit_bytes=56 * 2**20),
        name="solve",
    )(spectrum, forward, back, waves, waves)


def gather_kernel(planes, rows, points_ref, modes_y_ref, modes_z_ref, lines_ref, out_ref, plane):
    step = pl.program_id(0)
    chunk = CHUNK
    count = points_ref.shape[0] * points_ref.shape[2] // chunk
    first = pl.multiple_of(step * planes, 8)
    stack = jnp.concatenate([lines_ref[c, pl.ds(first, rows)] for c in range(3)], axis=0)
    if 3 * rows < LANES:
        stack = jnp.concatenate([stack, jnp.zeros((LANES - 3 * rows, COLS), F32)], axis=0)
    high, low = split(stack)
    plane[0:LANES] = high
    plane[LANES:] = low
    modes_y = [modes_y_ref[i] for i in range(7)]
    modes_z = [modes_z_ref[i] for i in range(7)]

    @pl.loop(0, count)
    def _(index):
        at = pl.ds(pl.multiple_of(index * chunk, chunk), chunk)
        points = chunk_of(points_ref, index)
        values, weights_x = column_values(points, modes_y, modes_z)
        highs, lows = [], []
        for value in values:
            h, l = split(value)
            highs.append(h)
            lows.append(l)
        result = jnp.dot(plane[...], jnp.concatenate(highs, axis=0), preferred_element_type=F32)
        small = jnp.dot(plane[0:LANES], jnp.concatenate(lows, axis=0), preferred_element_type=F32)
        result = result[:LANES] + result[LANES:] + small
        weight = plane_rows(points[3:4], weights_x, rows)
        out_ref[:, at] = jnp.concatenate(
            [
                jnp.sum(weight * result[c * rows : (c + 1) * rows], axis=0, keepdims=True)
                for c in range(3)
            ],
            axis=0,
        )


def gather(points, modes_y, modes_z, lines, planes, rows, joined):
    blocks, _, count = points.shape
    return pl.pallas_call(
        functools.partial(gather_kernel, planes, rows),
        grid=(blocks // joined,),
        in_specs=[
            pl.BlockSpec((joined, 9, count), lambda i: (i, 0, 0)),
            pl.BlockSpec(modes_y.shape, lambda i: (0, 0, 0)),
            pl.BlockSpec(modes_z.shape, lambda i: (0, 0, 0)),
            pl.BlockSpec(lines.shape, lambda i: (0, 0, 0)),
        ],
        out_specs=pl.BlockSpec((3, joined * count), lambda i: (0, i)),
        out_shape=jax.ShapeDtypeStruct((3, blocks * count), F32),
        scratch_shapes=[pltpu.VMEM((2 * LANES, COLS), BF16)],
        compiler_params=pltpu.CompilerParams(vmem_limit_bytes=56 * 2**20),
        name="interpolate",
    )(points, modes_y, modes_z, lines)


def line_tables():
    half = NX // 2
    place = np.arange(half)
    forward, back = [], []
    for parity in range(2):
        number = 2 * np.arange(NX // 4) + parity
        angle = (number[:, None] * place[None, :] % NX) * (2.0 * np.pi / NX)
        table = np.concatenate([np.cos(angle), np.sin(angle)], axis=0)
        for tables, value in ((forward, table), (back, table.T)):
            high = value.astype(ml_dtypes.bfloat16)
            low = (value - high.astype(np.float64)).astype(ml_dtypes.bfloat16)
            tables.append(np.concatenate([high, low, high], axis=1))
    return np.stack(forward), np.stack(back)


def mode_table(numbers, length):
    angle = numbers * (TWO_PI / length)
    rows = [numbers]
    for stencil in range(1, 4):
        rows += [jnp.cos(stencil * angle), jnp.sin(stencil * angle)]
    return jnp.broadcast_to(jnp.stack(rows)[:, :, None], (7, numbers.shape[0], LANES))


def far_tables(device, devices):
    quads = (NY // 2) * (NZ // 2) // devices
    own_y = quads // KZ
    parts_z = NZ // 2 // KZ
    first_y = (device // parts_z) * own_y
    first_z = (device % parts_z) * KZ
    local_y = jnp.arange(KY, dtype=jnp.int32)
    number_y = (first_y + local_y).astype(F32)
    number_z = (first_z + jnp.arange(KZ, dtype=jnp.int32)).astype(F32)
    modes_y = mode_table(number_y, NY)
    modes_z = mode_table(number_z, NZ)
    mult_y = jnp.where(local_y < own_y, jnp.where(number_y == 0, 1.0, 2.0), 0.0)
    mult_z = jnp.where(number_z == 0, 1.0, 2.0) / float(NX * NY * NZ)
    waves = jnp.stack(
        [
            jnp.repeat(number_y * (TWO_PI / NY), KZ),
            jnp.tile(number_z * (TWO_PI / NZ), KY),
            (mult_y[:, None] * mult_z[None, :]).reshape(-1),
        ]
    )
    waves = jnp.concatenate([waves, jnp.zeros((5, KY * KZ), F32)])
    return modes_y, modes_z, waves


def per_device(forces, stencil_start, fraction, tile_pairs, pair_count):
    groups = lax.axis_size("group")
    members = lax.axis_size("dev")
    devices = groups * members
    planes = NX // devices
    points = forces.shape[1]
    tiles = points // 128
    device = lax.axis_index("group") * members + lax.axis_index("dev")
    joined = max(1, 8 // planes)
    first_plane = (device // joined) * (joined * planes)
    start_x = (stencil_start[0:1] - first_plane).astype(F32)
    packed = jnp.concatenate(
        [forces, start_x, stencil_start[1:].astype(F32), fraction], axis=0
    )
    gathered = lax.all_gather(packed, ("group", "dev"))
    planes = planes * joined
    rows = (planes + 3 + 7) // 8 * 8
    modes_y, modes_z, waves = far_tables(device, devices)
    forward, back = line_tables()
    spectrum = spread(gathered, modes_y, modes_z, planes, rows, joined)
    lines = solve(spectrum, waves, jnp.asarray(forward), jnp.asarray(back))
    partial = gather(gathered, modes_y, modes_z, lines, planes, rows, joined)
    far = lax.psum_scatter(partial, ("group", "dev"), scatter_dimension=1, tiled=True)
    terms = pair_terms(stencil_start, fraction, forces, tile_pairs, pair_count[0])
    onehot = (tile_pairs[:, 0][:, None] == jnp.arange(tiles, dtype=jnp.int32)[None, :]).astype(
        jnp.float32
    )
    near = jnp.einsum("st,csp->ctp", onehot, terms, precision=lax.Precision.HIGHEST).reshape(
        3, points
    )
    return far + near


def solution(mesh):
    in_specs = (
        P(None, ("group", "dev")),
        P(None, ("group", "dev")),
        P(None, ("group", "dev")),
        P(("group", "dev"), None),
        P(("group", "dev")),
    )
    out_specs = P(None, ("group", "dev"))
    return jax.shard_map(
        per_device, mesh=mesh, in_specs=in_specs, out_specs=out_specs, check_vma=False
    )
```

time: 1010 us -> 631 us (0.62)
  matrix products: 371 us -> 0.15 us
  Pallas kernels: 0 us -> 173 us
  local copies, waits for them, and re-layouts: 131 us -> 29.4 us
  other arithmetic: 86.3 us -> 16.3 us
  starting transfers between devices: 54.3 us -> 0.04 us
  waiting for transfers between devices: 352 us -> 394 us
  between operations: 1.93 us -> 14.2 us
    dot_general x26 -> x0, matrix products: 371 us -> none  [the longest x20 180 us: apply_table(): return jnp.einsum(form, values, table, precision=lax.Precision.HIGHEST)]
    unnamed x0 -> x3, waiting for transfers between devices: none -> 342 us
    ppermute x6 -> x0, waiting for transfers between devices: 285 us -> none  [the longest x4 273 us: from_partner(): lax.ppermute(x, axis, [(i, i ^ 1 << bit) for i in range(lax.axis_size(axi...]
    pallas_call x0 -> x3, Pallas kernels: none -> 173 us  [the longest x1 79.5 us: spread(): pl.pallas_call(functools.partial(spread_kernel, planes, rows), grid=(bloc...]
    all_to_all x4 -> x0, waiting for transfers between devices: 66.8 us -> none  [the longest x1 38.7 us: per_device(): lax.all_to_all(imag_part, 'dev', split_axis=3, concat_axis=1, tiled=True)]
    all_gather x0 -> x1, waiting for transfers between devices: none -> 52.5 us  [per_device(): gathered = lax.all_gather(packed, ('group', 'dev'))]
    all_to_all x4 -> x0, other arithmetic: 43.6 us -> none  [the longest x1 11.8 us: per_device(): lax.all_to_all(imag_part, 'dev', split_axis=1, concat_axis=3, tiled=True)]
    all_to_all x4 -> x0, starting transfers between devices: 40.8 us -> none  [the longest x1 15.7 us: per_device(): lax.all_to_all(real_part, 'dev', split_axis=3, concat_axis=1, tiled=True)]
  transfers between devices with their start and end apart: 10 -> 2, of which waited for: 7 -> 2; matrix products, arithmetic and copies ran while one was open for 15% -> 4% of each run, Pallas kernels for 0% -> 0%
where the time goes in v1:
time: 631 us; the launch traced here: 627 us
  waiting for transfers between devices  394 us (62%)
  Pallas kernels  173 us (27%)
  local copies, waits for them, and re-layouts  29.4 us (5%)
  other arithmetic  16.3 us (3%)
  between operations  14.2 us (2%)
    unnamed x3, waiting for transfers between devices  342 us
    pallas_call x1, Pallas kernels, spread(): pl.pallas_call(functools.partial(spread_kernel, planes, rows), grid=(bloc...  79.5 us
    pallas_call x1, Pallas kernels, gather(): pl.pallas_call(functools.partial(gather_kernel, planes, rows), grid=(bloc...  72 us
    all_gather x1, waiting for transfers between devices, per_device(): gathered = lax.all_gather(packed, ('group', 'dev'))  52.5 us
    pallas_call x1, Pallas kernels, solve(): pl.pallas_call(functools.partial(solve_kernel, extra), in_specs=[full] *...  21 us
    unnamed x4, local copies, waits for them, and re-layouts  17.8 us
  transfers between devices with their start and end apart: 2, of which 2 were waited for; matrix products, arithmetic and copies ran while one was open for 4% of the time, Pallas kernels for 0%

profile of v1, /device:TPU:0, one launch (start us, length us, event | category | flops | bytes accessed | tf_op | source)
XLA Modules:
  0.0 627.0 jit_solution(8676365002626256326)
XLA Ops:
  6.5 0.8 slice_convert_fusion
  7.3 0.9 fusion.18
  8.2 1.5 maximum_bitcast_fusion
  9.8 0.8 slice_bitcast_fusion
  10.6 0.9 fusion.19
  11.5 0.6 gather_fusion.3
  12.0 0.6 gather_fusion.2
  13.8 0.6 gather_fusion.11
  14.4 0.6 gather_fusion.10
  16.7 0.6 gather_fusion
  19.6 0.6 gather_fusion.12
  20.2 0.6 gather_fusion.13
  21.8 0.7 maximum_maximum_fusion.waves_ref.scale_ref
  22.4 52.5 %all-gather.4.cloned.1.call-done.points_ref = f32[32,9,2048]{2,1,0:T(8,128)} async-done(((f32[1,9,2048]{2,1,0:T(8,128)}), f32[32,9,2048]{2,1,0:T(8,128)}) %all-gather.4.cloned.1.call-update) | async-done | bytes 2359312 | tf_op jit(solution)/shard_map/all_gather | solution.py:449
  75.0 0.7 broadcast_in_dim.22.modes_y_ref
  75.7 0.7 broadcast_in_dim.23.modes_z_ref
  76.4 79.5 %spread.1.spread_ref = f32[3,1032,512]{2,1,0:T(8,128)} custom-call(f32[32,9,2048]{2,1,0:T(8,128)} %all-gather.4.cloned.1.call-done.points_ref, f32[7,8,128]{2,1,0:T(8,128)} %broadcast_in_dim.22.modes_y_ref, f32[7,16,128]{2,1,0:T(8,128)} %broadcast_in_dim.23.modes_z_ref), custom_call_target="tpu_custom_call" | custom-call | tf_op jit(solution)/shard_map/spread/pallas_call | solution.py:208
  155.9 21.0 %solve.1.lines_ref = f32[3,1032,512]{2,1,0:T(8,128)} custom-call(f32[3,1032,512]{2,1,0:T(8,128)} %spread.1.spread_ref, bf16[2,512,1536]{2,1,0:T(8,128)(2,1)} %constant.98.clone.forward_ref, bf16[2,512,1536]{2,1,0:T(8,128)(2,1)} %constant.99.clone.back_ref, f32[8,128]{1,0:T(8,128)} %maximum_maximum_fusion.waves_ref.scale_ref, ...), custom_call_target="tpu_custom_call" | custom-call | tf_op jit(solution)/shard_map/solve/pallas_call | solution.py:318
  176.9 72.0 %interpolate.1 = f32[3,65536]{1,0:T(4,128)} custom-call(f32[32,9,2048]{2,1,0:T(8,128)} %all-gather.4.cloned.1.call-done.points_ref, f32[7,8,128]{2,1,0:T(8,128)} %broadcast_in_dim.22.modes_y_ref, f32[7,16,128]{2,1,0:T(8,128)} %broadcast_in_dim.23.modes_z_ref, f32[3,1032,512]{2,1,0:T(8,128)} %solve.1.lines_ref), custom_call_target="tpu_custom_call" | custom-call | tf_op jit(solution)/shard_map/interpolate/pallas_call | solution.py:371
  248.9 16.3 %copy.8 = f32[3,65536]{0,1:T(8,128)} copy(f32[3,65536]{1,0:T(4,128)} %interpolate.1) | data formatting | bytes 1572864
  265.2 10.6 %add_reduce_fusion.2 = (f32[48,128]{1,0:T(8,128)S(1)}, f32[48,128]{1,0:T(8,128)S(1)}, f32[48,128]{1,0:T(8,128)S(1)}) fusion(f32[48,128]{1,0:T(8,128)S(1)} %gather_fusion.12, f32[48,128]{1,0:T(8,128)S(1)} %gather_fusion.3, f32[48,128]{1,0:T(8,128)S(1)} %gather_fusion.2, s32[48,128]{1,0:T(8,128)S(1)} %gather_fusion.1, s32[48,128]{1,0:T(8,128)S(1)} %gather_fusion, ...), kind=kLoop, calls=%fused_computation.27 | loop fusion | flops 44808192 | bytes 442368 | tf_op jit(solution)/shard_map/reduce_sum | solution.py:64
  276.1 341.9 %reduce-scatter.4.cloned.1.call-done = f32[2048,3]{1,0:T(8,128)} async-done(((f32[65536,3]{1,0:T(8,128)}), f32[2048,3]{1,0:T(8,128)}) %reduce-scatter.4.cloned.1.call-update) | async-done | bytes 24592
  618.0 1.6 copy.9
  619.5 0.6 bitcast_add_fusion
  (39 shorter events, 5.8 us)
Async XLA Ops:
  6.5 13.0 %copy-start = (f32[3,2048]{1,0:T(4,128)S(1)}, f32[3,2048]{1,0:T(4,128)}, u32[]{:S(2)}) copy-start(f32[3,2048]{1,0:T(4,128)} %param.7) | copy-start | bytes 73732
  6.5 68.4 %all-gather.4.cloned.1.call-start = ((), (), s32[]{:S(2)}) async-start(), calls=%async_computation.1 | async-start | bytes 4325376 | tf_op jit(solution)/shard_map/all_gather | solution.py:449
  9.7 608.3 %reduce-scatter.4.cloned.1.call-start = ((), (), s32[]{:S(2)}) async-start(), calls=%async_computation.2 | async-start | bytes 34603008
Sparse Core Ops, SparseCore 0:
  10.2 64.7 all-gather.3
  265.3 352.5 reduce-scatter.3

commit v2 on v1

--- a/solution.py
+++ b/solution.py
@@ -20,9 +20,6 @@
 
 LANES = 128
 KZ = 16
-KY = 8
-COLS = 4 * KY * KZ
-CHUNK = 512
 BF16 = jnp.bfloat16
 F32 = jnp.float32
 
@@ -125,14 +122,15 @@
     return cosine * sum_cos - sine * sum_sin, sine * sum_cos + cosine * sum_sin
 
 
-def column_values(points, modes_y, modes_z):
-    weights = spline_weights(points[6:9])
-    rows_y = mode_rows(points[4:5], [w[1:2] for w in weights], modes_y, NY)
-    rows_z = mode_rows(points[5:6], [w[2:3] for w in weights], modes_z, NZ)
+def column_values(main, last, modes_y, modes_z):
+    weights = spline_weights(main[6:8])
+    weights_z = spline_weights(last)
+    rows_y = mode_rows(main[4:5], [w[1:2] for w in weights], modes_y, NY)
+    rows_z = mode_rows(main[5:6], weights_z, modes_z, NZ)
     values = []
     for ty in range(2):
         for tz in range(2):
-            for iy in range(KY):
+            for iy in range(rows_y[0].shape[0]):
                 values.append(rows_y[ty][iy : iy + 1] * rows_z[tz])
     return values, [w[0:1] for w in weights]
 
@@ -146,87 +144,77 @@
     return result
 
 
-def chunk_of(points_ref, index):
-    per_block = points_ref.shape[2] // CHUNK
-    at = pl.ds(pl.multiple_of(lax.rem(index, per_block) * CHUNK, CHUNK), CHUNK)
-    return points_ref[lax.div(index, per_block), :, at]
-
-
-def spread_kernel(planes, rows, points_ref, modes_y_ref, modes_z_ref, out_ref, acc):
-    step = pl.program_id(0)
-    chunk = CHUNK
-    count = points_ref.shape[0] * points_ref.shape[2] // chunk
-
-    @pl.when(step == 0)
-    def _():
-        out_ref[...] = jnp.zeros_like(out_ref)
-
+def first_plane(block, planes):
+    joined = max(1, 8 // planes)
+    return lax.div(block, joined) * (joined * planes)
+
+
+def spread_kernel(rows, main_ref, last_ref, modes_y_ref, modes_z_ref, out_ref):
+    main, last = main_ref[0], last_ref[0]
+    count = main.shape[1]
     modes_y = [modes_y_ref[i] for i in range(7)]
     modes_z = [modes_z_ref[i] for i in range(7)]
-
-    def one(index):
-        points = chunk_of(points_ref, index)
-        values, weights_x = column_values(points, modes_y, modes_z)
-        weight = plane_rows(points[3:4], weights_x, rows)
-        stack = jnp.concatenate([weight * points[c : c + 1] for c in range(3)], axis=0)
-        if 3 * rows < LANES:
-            stack = jnp.concatenate([stack, jnp.zeros((LANES - 3 * rows, chunk), F32)], axis=0)
-        high, low = split(stack)
-        both = jnp.concatenate([high, low], axis=0)
-        highs, lows = [], []
-        for value in values:
-            h, l = split(value)
-            highs.append(h)
-            lows.append(l)
-        left = jnp.concatenate([jnp.concatenate(highs, axis=0), jnp.concatenate(lows, axis=0)], axis=1)
-        right = jnp.concatenate([both, both], axis=1)
-        return lax.dot_general(
-            left, right, (((1,), (1,)), ((), ())), preferred_element_type=F32
-        )
-
-    acc[...] = jnp.zeros_like(acc)
-
-    @pl.loop(0, count)
-    def _(index):
-        acc[...] += one(index)
-
+    values, weights_x = column_values(main, last, modes_y, modes_z)
+    weight = plane_rows(main[3:4], weights_x, rows)
+    stack = jnp.concatenate([weight * main[c : c + 1] for c in range(3)], axis=0)
+    if 3 * rows < LANES:
+        stack = jnp.concatenate([stack, jnp.zeros((LANES - 3 * rows, count), F32)], axis=0)
+    both = jnp.concatenate(split(stack), axis=0)
+    parts = [split(value) for value in values]
+    left = jnp.concatenate(
+        [jnp.concatenate([p[i] for p in parts], axis=0) for i in range(2)], axis=1
+    )
+    right = jnp.concatenate([both, both], axis=1)
+    acc = lax.dot_general(left, right, (((1,), (1,)), ((), ())), preferred_element_type=F32)
     total = (acc[:, :LANES] + acc[:, LANES:]).T
-    first = pl.multiple_of(step * planes, 8)
-    for c in range(3):
-        out_ref[c, pl.ds(first, rows)] += total[c * rows : (c + 1) * rows]
-
-    @pl.when(step == pl.num_programs(0) - 1)
-    def _():
-        extra = out_ref.shape[1] - NX
-        for c in range(3):
-            out_ref[c, 0:extra] += out_ref[c, NX : NX + extra]
-
-
-def spread(points, modes_y, modes_z, planes, rows, joined):
-    blocks, _, count = points.shape
-    extra = rows - planes
+    out_ref[0] = total[: 3 * rows]
+
+
+def spread(points, modes_y, modes_z, rows):
+    main, last = points
+    blocks, _, count = main.shape
+    cols = 4 * modes_y.shape[1] * KZ
     return pl.pallas_call(
-        functools.partial(spread_kernel, planes, rows),
-        grid=(blocks // joined,),
+        functools.partial(spread_kernel, rows),
+        grid=(blocks,),
         in_specs=[
-            pl.BlockSpec((joined, 9, count), lambda i: (i, 0, 0)),
+            pl.BlockSpec((1, 8, count), lambda i: (i, 0, 0)),
+            pl.BlockSpec((1, 1, count), lambda i: (i, 0, 0)),
             pl.BlockSpec(modes_y.shape, lambda i: (0, 0, 0)),
             pl.BlockSpec(modes_z.shape, lambda i: (0, 0, 0)),
         ],
-        out_specs=pl.BlockSpec((3, NX + extra, COLS), lambda i: (0, 0, 0)),
-        out_shape=jax.ShapeDtypeStruct((3, NX + extra, COLS), F32),
-        scratch_shapes=[
-            pltpu.VMEM((COLS, 2 * LANES), F32),
-        ],
-        compiler_params=pltpu.CompilerParams(vmem_limit_bytes=56 * 2**20),
+        out_specs=pl.BlockSpec((1, 3 * rows, cols), lambda i: (i, 0, 0)),
+        out_shape=jax.ShapeDtypeStruct((blocks, 3 * rows, cols), F32),
+        compiler_params=pltpu.CompilerParams(vmem_limit_bytes=40 * 2**20),
+        cost_estimate=pl.CostEstimate(
+            flops=blocks * count * cols * LANES * 14,
+            bytes_accessed=blocks * (9 * count + 3 * rows * cols) * 4,
+            transcendentals=0,
+        ),
         name="spread",
-    )(points, modes_y, modes_z)
-
-
-def solve_kernel(extra, spread_ref, forward_ref, back_ref, waves_ref, scale_ref, out_ref, modes, stacked):
+    )(main, last, modes_y, modes_z)
+
+
+def solve_kernel(planes, rows, parts, ids_ref, *refs):
+    piece_refs = refs[:parts]
+    forward_ref, back_ref, waves_ref, out_ref, modes, stacked = refs[parts:]
+    extra = 8
+    out_ref[...] = jnp.zeros_like(out_ref)
+    before = 0
+    for piece_ref in piece_refs:
+
+        @pl.loop(0, piece_ref.shape[0])
+        def _(index):
+            first = pl.multiple_of(first_plane(ids_ref[before + index], planes), 8)
+            for c in range(3):
+                out_ref[c, pl.ds(first, rows)] += piece_ref[index, c * rows : (c + 1) * rows]
+
+        before += piece_ref.shape[0]
+    for c in range(3):
+        out_ref[c, 0:extra] += out_ref[c, NX : NX + extra]
     half = NX // 2
     quarter = NX // 4
-    lanes = COLS // 4
+    lanes = waves_ref.shape[1]
 
     def fill(value):
         high, low = split(value)
@@ -238,8 +226,8 @@
 
         @pl.loop(0, 3)
         def _(c):
-            first = spread_ref[c, 0:half]
-            second = spread_ref[c, half:NX]
+            first = out_ref[c, 0:half]
+            second = out_ref[c, half:NX]
             fill(first + second if parity == 0 else first - second)
             modes[parity, c] = jnp.dot(forward_ref[parity], stacked[...], preferred_element_type=F32)
 
@@ -312,52 +300,60 @@
         out_ref[c, NX : NX + extra] = out_ref[c, 0:extra]
 
 
-def solve(spectrum, waves, forward, back):
-    extra = spectrum.shape[1] - NX
+def solve(pieces, ids, waves, forward, back, planes, rows):
     full = pl.BlockSpec(memory_space=pltpu.VMEM)
+    cols = pieces[0].shape[2]
     return pl.pallas_call(
-        functools.partial(solve_kernel, extra),
-        in_specs=[full] * 5,
+        functools.partial(solve_kernel, planes, rows, len(pieces)),
+        in_specs=[pl.BlockSpec(memory_space=pltpu.SMEM)] + [full] * (len(pieces) + 3),
         out_specs=full,
-        out_shape=jax.ShapeDtypeStruct(spectrum.shape, F32),
+        out_shape=jax.ShapeDtypeStruct((3, NX + 8, cols), F32),
         scratch_shapes=[
-            pltpu.VMEM((2, 3, NX // 2, COLS), F32),
-            pltpu.VMEM((3 * NX // 2, COLS), BF16),
+            pltpu.VMEM((2, 3, NX // 2, cols), F32),
+            pltpu.VMEM((3 * NX // 2, cols), BF16),
         ],
         compiler_params=pltpu.CompilerParams(vmem_limit_bytes=56 * 2**20),
+        cost_estimate=pl.CostEstimate(
+            flops=36 * NX // 2 * NX // 2 * cols,
+            bytes_accessed=6 * NX * cols * 4,
+            transcendentals=0,
+        ),
         name="solve",
-    )(spectrum, forward, back, waves, waves)
-
-
-def gather_kernel(planes, rows, points_ref, modes_y_ref, modes_z_ref, lines_ref, out_ref, plane):
+    )(ids, *pieces, forward, back, waves)
+
+
+def gather_kernel(planes, rows, parts, ids_ref, *refs):
+    mains, lasts = refs[:parts], refs[parts : 2 * parts]
+    modes_y_ref, modes_z_ref, lines_ref, out_ref, plane = refs[2 * parts :]
     step = pl.program_id(0)
-    chunk = CHUNK
-    count = points_ref.shape[0] * points_ref.shape[2] // chunk
-    first = pl.multiple_of(step * planes, 8)
+    each = pl.num_programs(0) // parts
+    first = pl.multiple_of(first_plane(ids_ref[step], planes), 8)
     stack = jnp.concatenate([lines_ref[c, pl.ds(first, rows)] for c in range(3)], axis=0)
     if 3 * rows < LANES:
-        stack = jnp.concatenate([stack, jnp.zeros((LANES - 3 * rows, COLS), F32)], axis=0)
+        stack = jnp.concatenate([stack, jnp.zeros((LANES - 3 * rows, lines_ref.shape[2]), F32)], axis=0)
     high, low = split(stack)
     plane[0:LANES] = high
     plane[LANES:] = low
     modes_y = [modes_y_ref[i] for i in range(7)]
     modes_z = [modes_z_ref[i] for i in range(7)]
-
-    @pl.loop(0, count)
-    def _(index):
-        at = pl.ds(pl.multiple_of(index * chunk, chunk), chunk)
-        points = chunk_of(points_ref, index)
-        values, weights_x = column_values(points, modes_y, modes_z)
-        highs, lows = [], []
-        for value in values:
-            h, l = split(value)
-            highs.append(h)
-            lows.append(l)
-        result = jnp.dot(plane[...], jnp.concatenate(highs, axis=0), preferred_element_type=F32)
-        small = jnp.dot(plane[0:LANES], jnp.concatenate(lows, axis=0), preferred_element_type=F32)
+    main, last = mains[0][0], lasts[0][0]
+    for part in range(1, parts):
+        here = step >= part * each
+        main = jnp.where(here, mains[part][0], main)
+        last = jnp.where(here, lasts[part][0], last)
+    count = main.shape[1]
+    chunk = count // 4
+    for index in range(4):
+        at = slice(index * chunk, (index + 1) * chunk)
+        values, weights_x = column_values(main[:, at], last[:, at], modes_y, modes_z)
+        pairs = [split(value) for value in values]
+        highs = jnp.concatenate([p[0] for p in pairs], axis=0)
+        lows = jnp.concatenate([p[1] for p in pairs], axis=0)
+        result = jnp.dot(plane[...], highs, preferred_element_type=F32)
+        small = jnp.dot(plane[0:LANES], lows, preferred_element_type=F32)
         result = result[:LANES] + result[LANES:] + small
-        weight = plane_rows(points[3:4], weights_x, rows)
-        out_ref[:, at] = jnp.concatenate(
+        weight = plane_rows(main[3:4, at], weights_x, rows)
+        out_ref[0, :, at] = jnp.concatenate(
             [
                 jnp.sum(weight * result[c * rows : (c + 1) * rows], axis=0, keepdims=True)
                 for c in range(3)
@@ -366,23 +362,41 @@
         )
 
 
-def gather(points, modes_y, modes_z, lines, planes, rows, joined):
-    blocks, _, count = points.shape
+def gather(points, ids, modes_y, modes_z, lines, planes, rows):
+    parts = len(points)
+    mains = [p[0] for p in points]
+    lasts = [p[1] for p in points]
+    each, _, count = mains[0].shape
+    blocks = parts * each
+    cols = lines.shape[2]
+
+    def at(part):
+        return lambda i, ids: (jnp.clip(i - part * each, 0, each - 1), 0, 0)
+
     return pl.pallas_call(
-        functools.partial(gather_kernel, planes, rows),
-        grid=(blocks // joined,),
-        in_specs=[
-            pl.BlockSpec((joined, 9, count), lambda i: (i, 0, 0)),
-            pl.BlockSpec(modes_y.shape, lambda i: (0, 0, 0)),
-            pl.BlockSpec(modes_z.shape, lambda i: (0, 0, 0)),
-            pl.BlockSpec(lines.shape, lambda i: (0, 0, 0)),
-        ],
-        out_specs=pl.BlockSpec((3, joined * count), lambda i: (0, i)),
-        out_shape=jax.ShapeDtypeStruct((3, blocks * count), F32),
-        scratch_shapes=[pltpu.VMEM((2 * LANES, COLS), BF16)],
-        compiler_params=pltpu.CompilerParams(vmem_limit_bytes=56 * 2**20),
+        functools.partial(gather_kernel, planes, rows, parts),
+        grid_spec=pltpu.PrefetchScalarGridSpec(
+            num_scalar_prefetch=1,
+            grid=(blocks,),
+            in_specs=[pl.BlockSpec((1, 8, count), at(part)) for part in range(parts)]
+            + [pl.BlockSpec((1, 1, count), at(part)) for part in range(parts)]
+            + [
+                pl.BlockSpec(modes_y.shape, lambda i, ids: (0, 0, 0)),
+                pl.BlockSpec(modes_z.shape, lambda i, ids: (0, 0, 0)),
+                pl.BlockSpec(lines.shape, lambda i, ids: (0, 0, 0)),
+            ],
+            out_specs=pl.BlockSpec((1, 3, count), lambda i, ids: (ids[i], 0, 0)),
+            scratch_shapes=[pltpu.VMEM((2 * LANES, cols), BF16)],
+        ),
+        out_shape=jax.ShapeDtypeStruct((blocks, 3, count), F32),
+        compiler_params=pltpu.CompilerParams(vmem_limit_bytes=48 * 2**20),
+        cost_estimate=pl.CostEstimate(
+            flops=blocks * count * cols * LANES * 14,
+            bytes_accessed=blocks * 12 * count * 4,
+            transcendentals=0,
+        ),
         name="interpolate",
-    )(points, modes_y, modes_z, lines)
+    )(ids, *mains, *lasts, modes_y, modes_z, lines)
 
 
 def line_tables():
@@ -414,21 +428,21 @@
     parts_z = NZ // 2 // KZ
     first_y = (device // parts_z) * own_y
     first_z = (device % parts_z) * KZ
-    local_y = jnp.arange(KY, dtype=jnp.int32)
+    local_y = jnp.arange(own_y, dtype=jnp.int32)
     number_y = (first_y + local_y).astype(F32)
     number_z = (first_z + jnp.arange(KZ, dtype=jnp.int32)).astype(F32)
     modes_y = mode_table(number_y, NY)
     modes_z = mode_table(number_z, NZ)
-    mult_y = jnp.where(local_y < own_y, jnp.where(number_y == 0, 1.0, 2.0), 0.0)
+    mult_y = jnp.where(number_y == 0, 1.0, 2.0)
     mult_z = jnp.where(number_z == 0, 1.0, 2.0) / float(NX * NY * NZ)
     waves = jnp.stack(
         [
             jnp.repeat(number_y * (TWO_PI / NY), KZ),
-            jnp.tile(number_z * (TWO_PI / NZ), KY),
+            jnp.tile(number_z * (TWO_PI / NZ), own_y),
             (mult_y[:, None] * mult_z[None, :]).reshape(-1),
         ]
     )
-    waves = jnp.concatenate([waves, jnp.zeros((5, KY * KZ), F32)])
+    waves = jnp.concatenate([waves, jnp.zeros((5, own_y * KZ), F32)])
     return modes_y, modes_z, waves
 
 
@@ -440,21 +454,40 @@
     points = forces.shape[1]
     tiles = points // 128
     device = lax.axis_index("group") * members + lax.axis_index("dev")
-    joined = max(1, 8 // planes)
-    first_plane = (device // joined) * (joined * planes)
-    start_x = (stencil_start[0:1] - first_plane).astype(F32)
-    packed = jnp.concatenate(
-        [forces, start_x, stencil_start[1:].astype(F32), fraction], axis=0
-    )
-    gathered = lax.all_gather(packed, ("group", "dev"))
-    planes = planes * joined
-    rows = (planes + 3 + 7) // 8 * 8
+    rows = max(8, planes) + 8
+    start_x = (stencil_start[0:1] - first_plane(device, planes)).astype(F32)
+    main = jnp.concatenate(
+        [forces, start_x, stencil_start[1:].astype(F32), fraction[0:2]], axis=0
+    )
+    own = (main[None], fraction[2:3][None])
+
+    def from_flipped(values, mask):
+        pairs = [(i, i ^ mask) for i in range(devices)]
+        return jax.tree.map(lambda v: lax.ppermute(v, ("group", "dev"), pairs), values)
+
+    def join(*values):
+        return jax.tree.map(lambda *v: jnp.concatenate(v, axis=0), *values)
+
+    near_blocks = join(own, *[from_flipped(own, mask) for mask in (4, 8, 12)])
+    masks = [0, 4, 8, 12]
+    last_bit = devices.bit_length() - 2
+    for bit in [1] + list(range(4, last_bit)):
+        near_blocks = join(near_blocks, from_flipped(near_blocks, 1 << bit))
+        masks = masks + [m ^ 1 << bit for m in masks]
+    core = from_flipped(near_blocks, 1)
+    other = from_flipped(near_blocks, 1 << last_bit)
+    blocks = [near_blocks, core, other, from_flipped(other, 1)]
+    masks = np.array(
+        [m ^ flip for flip in (0, 1, 1 << last_bit, 1 << last_bit ^ 1) for m in masks], np.int32
+    )
+    ids = device ^ jnp.asarray(masks)
     modes_y, modes_z, waves = far_tables(device, devices)
     forward, back = line_tables()
-    spectrum = spread(gathered, modes_y, modes_z, planes, rows, joined)
-    lines = solve(spectrum, waves, jnp.asarray(forward), jnp.asarray(back))
-    partial = gather(gathered, modes_y, modes_z, lines, planes, rows, joined)
-    far = lax.psum_scatter(partial, ("group", "dev"), scatter_dimension=1, tiled=True)
+    pieces = [spread(points_of, modes_y, modes_z, rows) for points_of in blocks]
+    lines = solve(pieces, ids, waves, jnp.asarray(forward), jnp.asarray(back), planes, rows)
+    partial = gather(blocks, ids, modes_y, modes_z, lines, planes, rows)
+    shares = lax.all_to_all(partial, ("group", "dev"), 0, 0, tiled=True)
+    far = jnp.sum(shares, axis=0)
     terms = pair_terms(stencil_start, fraction, forces, tile_pairs, pair_count[0])
     onehot = (tile_pairs[:, 0][:, None] == jnp.arange(tiles, dtype=jnp.int32)[None, :]).astype(
         jnp.float32

time: 631 us -> 218 us (0.35)
  waiting for transfers between devices: 394 us -> 25.8 us
  Pallas kernels: 173 us -> 133 us
  starting transfers between devices: 0.04 us -> 22.1 us
  between operations: 14.2 us -> 0.88 us
  local copies, waits for them, and re-layouts: 29.4 us -> 17.9 us
    unnamed x3 -> x0, waiting for transfers between devices: 342 us -> none
    all_gather x1 -> x0, waiting for transfers between devices: 52.5 us -> none  [per_device(): gathered = lax.all_gather(packed, ('group', 'dev'))]
    pallas_call x3 -> x6, Pallas kernels: 173 us -> 133 us  [the longest x1 59.2 us: gather(): pl.pallas_call(functools.partial(gather_kernel, planes, rows, parts), gri...]
    all_to_all x0 -> x1, waiting for transfers between devices: none -> 16.3 us  [per_device(): shares = lax.all_to_all(partial, ('group', 'dev'), 0, 0, tiled=True)]
    ppermute x0 -> x14, starting transfers between devices: none -> 16.1 us  [from_flipped(): lax.ppermute(v, ('group', 'dev'), pairs)]
    unnamed x4 -> x17, local copies, waits for them, and re-layouts: 17.8 us -> 6 us
    ppermute x0 -> x14, waiting for transfers between devices: none -> 9.47 us  [from_flipped(): lax.ppermute(v, ('group', 'dev'), pairs)]
  transfers between devices with their start and end apart: 2 -> 15, of which waited for: 2 -> 4; matrix products, arithmetic and copies ran while one was open for 4% -> 13% of each run, Pallas kernels for 0% -> 18%
where the time goes in v2:
time: 218 us; the launch traced here: 217 us
  Pallas kernels  133 us (61%)
  waiting for transfers between devices  25.8 us (12%)
  starting transfers between devices  22.1 us (10%)
  local copies, waits for them, and re-layouts  17.9 us (8%)
  other arithmetic  17.1 us (8%)
    pallas_call x1, Pallas kernels, gather(): pl.pallas_call(functools.partial(gather_kernel, planes, rows, parts), gri...  59.2 us
    pallas_call x4, Pallas kernels, spread(): pl.pallas_call(functools.partial(spread_kernel, rows), grid=(blocks,), in...  51.1 us
    pallas_call x1, Pallas kernels, solve(): pl.pallas_call(functools.partial(solve_kernel, planes, rows, len(pieces))...  22.8 us
    all_to_all x1, waiting for transfers between devices, per_device(): shares = lax.all_to_all(partial, ('group', 'dev'), 0, 0, tiled=True)  16.3 us
    ppermute x14, starting transfers between devices, from_flipped(): lax.ppermute(v, ('group', 'dev'), pairs)  16.1 us
    reduce_sum x1, other arithmetic, pair_terms(): jnp.sum(diagonal * pulled[component] + falloff * deltas[component] * alon...  10.6 us
    ppermute x14, waiting for transfers between devices, from_flipped(): lax.ppermute(v, ('group', 'dev'), pairs)  9.47 us
    unnamed x17, local copies, waits for them, and re-layouts  6 us
  transfers between devices with their start and end apart: 15, of which 4 were waited for; matrix products, arithmetic and copies ran while one was open for 13% of the time, Pallas kernels for 18%

profile of v2, /device:TPU:0, one launch (start us, length us, event | category | flops | bytes accessed | tf_op | source)
XLA Modules:
  0.0 217.1 jit_solution(1070676744615616754)
XLA Ops:
  0.9 5.1 %collective-permute-start.9 = (f32[1,1,2048]{2,1,0:T(1,128)S(1)}, f32[1,1,2048]{2,1,0:T(1,128)S(1)}, u32[]{:S(2)}, u32[]{:S(2)}) collective-permute-start(f32[1,1,2048]{2,1,0:T(1,128)S(1)} %get-tuple-element.18), channel_id=1, source_target_pairs={{0,12},{1,13},{2,14},{3,15},{4,8},{5,9},{6,10},{7,11},{8,4},{9,5},... | collective-permute-start | bytes 24584 | tf_op jit(solution)/shard_map/ppermute | solution.py:466
  8.2 0.9 fusion.18
  9.9 3.8 %collective-permute-start.2 = (f32[1,8,2048]{2,1,0:T(8,128)S(1)}, f32[1,8,2048]{2,1,0:T(8,128)S(1)}, u32[]{:S(2)}, u32[]{:S(2)}) collective-permute-start(f32[1,8,2048]{2,1,0:T(8,128)S(1)} %get-tuple-element.9), channel_id=1, source_target_pairs={{0,12},{1,13},{2,14},{3,15},{4,8},{5,9},{6,10},{7,11},{8,4},{9,5},... | collective-permute-start | bytes 196616 | tf_op jit(solution)/shard_map/ppermute | solution.py:466
  14.1 0.9 fusion.17
  16.4 1.3 broadcast_xor_fusion.ids_ref
  29.1 1.7 collective-permute-start.10
  30.8 2.3 %collective-permute-done.10 = f32[4,1,2048]{2,1,0:T(1,128)S(1)} collective-permute-done((f32[4,1,2048]{2,1,0:T(1,128)S(1)}, f32[4,1,2048]{2,1,0:T(1,128)S(1)}, u32[]{:S(2)}, u32[]{:S(2)}) %collective-permute-start.10) | collective-permute-done | bytes 32800 | tf_op jit(solution)/shard_map/ppermute | solution.py:466
  33.1 1.7 collective-permute-start.12
  34.8 1.6 collective-permute-start.3
  36.4 1.0 collective-permute-done.12.last_ref.refs_6_
  37.4 6.2 %collective-permute-done.3 = f32[4,8,2048]{2,1,0:T(8,128)S(1)} collective-permute-done((f32[4,8,2048]{2,1,0:T(8,128)S(1)}, f32[4,8,2048]{2,1,0:T(8,128)S(1)}, u32[]{:S(2)}, u32[]{:S(2)}) %collective-permute-start.3) | collective-permute-done | bytes 262176 | tf_op jit(solution)/shard_map/ppermute | solution.py:466
  44.2 12.8 %spread.4.refs_0_ = f32[8,120,512]{2,1,0:T(8,128)S(1)} custom-call(f32[8,8,2048]{2,1,0:T(8,128)S(1)} %constant_dynamic-update-slice_fusion.main_ref.refs_0_, f32[8,1,2048]{2,1,0:T(1,128)S(1)} %constant_dynamic-update-slice_fusion.5.last_ref.refs_4_, f32[7,8,128]{2,1,0:T(8,128)S(1)} %broadcast_in_dim.26.modes_y_ref.refs_8_, ...), custom_call_target="tpu_custom_call" | custom-call | flops 15032385536 | bytes 2555904 | tf_op jit(solution)/shard_map/spread/pallas_call | solution.py:177
  57.0 1.3 copy-done
  58.9 12.7 %spread.6.refs_2_ = f32[8,120,512]{2,1,0:T(8,128)S(1)} custom-call(f32[8,8,2048]{2,1,0:T(8,128)S(1)} %collective-permute-done.5.main_ref.refs_2_, f32[8,1,2048]{2,1,0:T(1,128)S(1)} %collective-permute-done.12.last_ref.refs_6_, f32[7,8,128]{2,1,0:T(8,128)S(1)} %broadcast_in_dim.26.modes_y_ref.refs_8_, f32[7,16,128]{2,1,0:T(8,128)S(1)} %broadcast_in_dim.27.modes_z_ref.refs_9_), custom_call_target="tpu_custom_call" | custom-call | flops 15032385536 | bytes 2555904 | tf_op jit(solution)/shard_map/spread/pallas_call | solution.py:177
  71.6 1.3 copy-done.1
  72.9 12.7 %spread.5.refs_1_ = f32[8,120,512]{2,1,0:T(8,128)S(1)} custom-call(f32[8,8,2048]{2,1,0:T(8,128)S(1)} %collective-permute-done.4.main_ref.refs_1_, f32[8,1,2048]{2,1,0:T(1,128)S(1)} %collective-permute-done.11.last_ref.refs_5_, f32[7,8,128]{2,1,0:T(8,128)S(1)} %broadcast_in_dim.26.modes_y_ref.refs_8_, f32[7,16,128]{2,1,0:T(8,128)S(1)} %broadcast_in_dim.27.modes_z_ref.refs_9_), custom_call_target="tpu_custom_call" | custom-call | flops 15032385536 | bytes 2555904 | tf_op jit(solution)/shard_map/spread/pallas_call | solution.py:177
  85.6 1.3 copy-done.2
  87.0 12.7 %spread.7.refs_3_ = f32[8,120,512]{2,1,0:T(8,128)S(1)} custom-call(f32[8,8,2048]{2,1,0:T(8,128)S(1)} %collective-permute-done.6.main_ref.refs_3_, f32[8,1,2048]{2,1,0:T(1,128)S(1)} %collective-permute-done.13.last_ref.refs_7_, f32[7,8,128]{2,1,0:T(8,128)S(1)} %broadcast_in_dim.26.modes_y_ref.refs_8_, f32[7,16,128]{2,1,0:T(8,128)S(1)} %broadcast_in_dim.27.modes_z_ref.refs_9_), custom_call_target="tpu_custom_call" | custom-call | flops 15032385536 | bytes 2555904 | tf_op jit(solution)/shard_map/spread/pallas_call | solution.py:177
  99.7 1.3 copy-done.3
  101.0 22.8 %solve.1.refs_10_ = f32[3,1032,512]{2,1,0:T(8,128)} custom-call(s32[32]{0:T(128)} %broadcast_xor_fusion.ids_ref, f32[8,120,512]{2,1,0:T(8,128)} %copy-done, f32[8,120,512]{2,1,0:T(8,128)} %copy-done.2, f32[8,120,512]{2,1,0:T(8,128)} %copy-done.1, f32[8,120,512]{2,1,0:T(8,128)} %copy-done.3, bf16[2,512,1536]{2,1,0:T(8,128)(2,1)} %constant.92.clone.refs_4_, ...), custom_call_target="tpu_custom_call" | custom-call | flops 4831838208 | bytes 12582912 | tf_op jit(solution)/shard_map/solve/pallas_call | solution.py:306
  123.9 59.2 %interpolate.1 = f32[32,3,2048]{2,1,0:T(4,128)} custom-call(s32[32]{0:T(128)S(1)} %copy-done.4, f32[8,8,2048]{2,1,0:T(8,128)S(1)} %constant_dynamic-update-slice_fusion.main_ref.refs_0_, f32[8,8,2048]{2,1,0:T(8,128)S(1)} %collective-permute-done.4.main_ref.refs_1_, f32[8,8,2048]{2,1,0:T(8,128)S(1)} %collective-permute-done.5.main_ref.refs_2_, ...), custom_call_target="tpu_custom_call" | custom-call | flops 60129542144 | bytes 3145728 | tf_op jit(solution)/shard_map/interpolate/pallas_call | solution.py:376
  183.1 6.0 %all-to-all-start = ((f32[32,3,2048]{2,1,0:T(4,128)}), f32[32,3,2048]{2,1,0:T(4,128)S(1)}, u32[]{:S(2)}, u32[]{:S(2)}) async-start(f32[32,3,2048]{2,1,0:T(4,128)} %interpolate.1), calls=%async_computation | async-start | bytes 2097152 | tf_op jit(solution)/shard_map/all_to_all | solution.py:489
  189.1 10.6 %add_reduce_fusion.2 = (f32[48,128]{1,0:T(8,128)S(1)}, f32[48,128]{1,0:T(8,128)S(1)}, f32[48,128]{1,0:T(8,128)S(1)}) fusion(f32[48,128]{1,0:T(8,128)S(1)} %gather_fusion.12, f32[48,128]{1,0:T(8,128)S(1)} %gather_fusion.3, f32[48,128]{1,0:T(8,128)S(1)} %gather_fusion.2, s32[48,128]{1,0:T(8,128)S(1)} %gather_fusion.1, s32[48,128]{1,0:T(8,128)S(1)} %gather_fusion, ...), kind=kLoop, calls=%fused_computation.27 | loop fusion | flops 44808192 | bytes 442368 | tf_op jit(solution)/shard_map/reduce_sum | solution.py:61
  199.9 16.3 %all-to-all-done = f32[32,3,2048]{2,1,0:T(4,128)S(1)} async-done(((f32[32,3,2048]{2,1,0:T(4,128)}), f32[32,3,2048]{2,1,0:T(4,128)S(1)}, u32[]{:S(2)}, u32[]{:S(2)}) %all-to-all-start) | async-done | bytes 786464 | tf_op jit(solution)/shard_map/all_to_all | solution.py:489
  (86 shorter events, 18.6 us)
Async XLA Ops:
  0.9 27.5 %collective-permute-start.9 = (f32[1,1,2048]{2,1,0:T(1,128)S(1)}, f32[1,1,2048]{2,1,0:T(1,128)S(1)}, u32[]{:S(2)}, u32[]{:S(2)}) collective-permute-start(f32[1,1,2048]{2,1,0:T(1,128)S(1)} %get-tuple-element.18), channel_id=1, source_target_pairs={{0,12},{1,13},{2,14},{3,15},{4,8},{5,9},{6,10},{7,11},{8,4},{9,5},... | collective-permute-start | bytes 24584 | tf_op jit(solution)/shard_map/ppermute | solution.py:466
  6.0 23.0 %collective-permute-start.8 = (f32[1,1,2048]{2,1,0:T(1,128)S(1)}, f32[1,1,2048]{2,1,0:T(1,128)S(1)}, u32[]{:S(2)}, u32[]{:S(2)}) collective-permute-start(f32[1,1,2048]{2,1,0:T(1,128)S(1)} %get-tuple-element.18), channel_id=1, source_target_pairs={{0,8},{1,9},{2,10},{3,11},{4,12},{5,13},{6,14},{7,15},{8,0},{9,1},... | collective-permute-start | bytes 24584 | tf_op jit(solution)/shard_map/ppermute | solution.py:466
  6.0 23.0 %collective-permute-start.7 = (f32[1,1,2048]{2,1,0:T(1,128)S(1)}, f32[1,1,2048]{2,1,0:T(1,128)S(1)}, u32[]{:S(2)}, u32[]{:S(2)}) collective-permute-start(f32[1,1,2048]{2,1,0:T(1,128)S(1)} %get-tuple-element.18), channel_id=1, source_target_pairs={{0,4},{1,5},{2,6},{3,7},{4,0},{5,1},{6,2},{7,3},{8,12},{9,13},{10,... | collective-permute-start | bytes 24584 | tf_op jit(solution)/shard_map/ppermute | solution.py:466
  9.9 24.9 %collective-permute-start.2 = (f32[1,8,2048]{2,1,0:T(8,128)S(1)}, f32[1,8,2048]{2,1,0:T(8,128)S(1)}, u32[]{:S(2)}, u32[]{:S(2)}) collective-permute-start(f32[1,8,2048]{2,1,0:T(8,128)S(1)} %get-tuple-element.9), channel_id=1, source_target_pairs={{0,12},{1,13},{2,14},{3,15},{4,8},{5,9},{6,10},{7,11},{8,4},{9,5},... | collective-permute-start | bytes 196616 | tf_op jit(solution)/shard_map/ppermute | solution.py:466
  13.7 21.1 %collective-permute-start.1 = (f32[1,8,2048]{2,1,0:T(8,128)S(1)}, f32[1,8,2048]{2,1,0:T(8,128)S(1)}, u32[]{:S(2)}, u32[]{:S(2)}) collective-permute-start(f32[1,8,2048]{2,1,0:T(8,128)S(1)} %get-tuple-element.9), channel_id=1, source_target_pairs={{0,8},{1,9},{2,10},{3,11},{4,12},{5,13},{6,14},{7,15},{8,0},{9,1},... | collective-permute-start | bytes 196616 | tf_op jit(solution)/shard_map/ppermute | solution.py:466
  28.4 6.4 %collective-permute-start = (f32[1,8,2048]{2,1,0:T(8,128)S(1)}, f32[1,8,2048]{2,1,0:T(8,128)S(1)}, u32[]{:S(2)}, u32[]{:S(2)}) collective-permute-start(f32[1,8,2048]{2,1,0:T(8,128)S(1)} %get-tuple-element.9), channel_id=1, source_target_pairs={{0,4},{1,5},{2,6},{3,7},{4,0},{5,1},{6,2},{7,3},{8,12},{9,13},{10,... | collective-permute-start | bytes 196616 | tf_op jit(solution)/shard_map/ppermute | solution.py:466
  29.1 4.0 %collective-permute-start.10 = (f32[4,1,2048]{2,1,0:T(1,128)S(1)}, f32[4,1,2048]{2,1,0:T(1,128)S(1)}, u32[]{:S(2)}, u32[]{:S(2)}) collective-permute-start(f32[4,1,2048]{2,1,0:T(1,128)S(1)} %pad_maximum_fusion.1), channel_id=1, source_target_pairs={{0,2},{1,3},{2,0},{3,1},{4,6},{5,7},{6,4},{7,5},{8,10},{9,11},{10,... | collective-permute-start | bytes 98312 | tf_op jit(solution)/shard_map/ppermute | solution.py:466
  33.1 4.3 %collective-permute-start.12 = (f32[8,1,2048]{2,1,0:T(1,128)S(1)}, f32[8,1,2048]{2,1,0:T(1,128)S(1)}, u32[]{:S(2)}, u32[]{:S(2)}) collective-permute-start(f32[8,1,2048]{2,1,0:T(1,128)S(1)} %constant_dynamic-update-slice_fusion.5.last_ref.refs_4_), channel_id=1, source_target_pairs={{0,16},{1,17},{2,18},{3,19},{4,20},{5,21},{6,22},{7,23},{8,24},{9,... | collective-permute-start | bytes 196616 | tf_op jit(solution)/shard_map/ppermute | solution.py:466
  34.8 38.1 %collective-permute-start.11 = (f32[8,1,2048]{2,1,0:T(1,128)S(1)}, f32[8,1,2048]{2,1,0:T(1,128)S(1)}, u32[]{:S(2)}, u32[]{:S(2)}) collective-permute-start(f32[8,1,2048]{2,1,0:T(1,128)S(1)} %constant_dynamic-update-slice_fusion.5.last_ref.refs_4_), channel_id=1, source_target_pairs={{0,1},{1,0},{2,3},{3,2},{4,5},{5,4},{6,7},{7,6},{8,9},{9,8},{10,11... | collective-permute-start | bytes 196616 | tf_op jit(solution)/shard_map/ppermute | solution.py:466
  34.8 8.8 %collective-permute-start.3 = (f32[4,8,2048]{2,1,0:T(8,128)S(1)}, f32[4,8,2048]{2,1,0:T(8,128)S(1)}, u32[]{:S(2)}, u32[]{:S(2)}) collective-permute-start(f32[4,8,2048]{2,1,0:T(8,128)S(1)} %pad_maximum_fusion), channel_id=1, source_target_pairs={{0,2},{1,3},{2,0},{3,1},{4,6},{5,7},{6,4},{7,5},{8,10},{9,11},{10,... | collective-permute-start | bytes 786440 | tf_op jit(solution)/shard_map/ppermute | solution.py:466
  37.4 49.6 %collective-permute-start.13 = (f32[8,1,2048]{2,1,0:T(1,128)S(1)}, f32[8,1,2048]{2,1,0:T(1,128)S(1)}, u32[]{:S(2)}, u32[]{:S(2)}) collective-permute-start(f32[8,1,2048]{2,1,0:T(1,128)S(1)} %collective-permute-done.12.last_ref.refs_6_), channel_id=1, source_target_pairs={{0,1},{1,0},{2,3},{3,2},{4,5},{5,4},{6,7},{7,6},{8,9},{9,8},{10,11... | collective-permute-start | bytes 196616 | tf_op jit(solution)/shard_map/ppermute | solution.py:466
  43.6 14.8 %collective-permute-start.5 = (f32[8,8,2048]{2,1,0:T(8,128)S(1)}, f32[8,8,2048]{2,1,0:T(8,128)S(1)}, u32[]{:S(2)}, u32[]{:S(2)}) collective-permute-start(f32[8,8,2048]{2,1,0:T(8,128)S(1)} %constant_dynamic-update-slice_fusion.main_ref.refs_0_), channel_id=1, source_target_pairs={{0,16},{1,17},{2,18},{3,19},{4,20},{5,21},{6,22},{7,23},{8,24},{9,... | collective-permute-start | bytes 1572872 | tf_op jit(solution)/shard_map/ppermute | solution.py:466
  44.0 28.9 %collective-permute-start.4 = (f32[8,8,2048]{2,1,0:T(8,128)S(1)}, f32[8,8,2048]{2,1,0:T(8,128)S(1)}, u32[]{:S(2)}, u32[]{:S(2)}) collective-permute-start(f32[8,8,2048]{2,1,0:T(8,128)S(1)} %constant_dynamic-update-slice_fusion.main_ref.refs_0_), channel_id=1, source_target_pairs={{0,1},{1,0},{2,3},{3,2},{4,5},{5,4},{6,7},{7,6},{8,9},{9,8},{10,11... | collective-permute-start | bytes 1572872 | tf_op jit(solution)/shard_map/ppermute | solution.py:466
  57.0 1.3 copy-start
  58.4 28.6 %collective-permute-start.6 = (f32[8,8,2048]{2,1,0:T(8,128)S(1)}, f32[8,8,2048]{2,1,0:T(8,128)S(1)}, u32[]{:S(2)}, u32[]{:S(2)}) collective-permute-start(f32[8,8,2048]{2,1,0:T(8,128)S(1)} %collective-permute-done.5.main_ref.refs_2_), channel_id=1, source_target_pairs={{0,1},{1,0},{2,3},{3,2},{4,5},{5,4},{6,7},{7,6},{8,9},{9,8},{10,11... | collective-permute-start | bytes 1572872 | tf_op jit(solution)/shard_map/ppermute | solution.py:466
  71.6 1.3 copy-start.1
  85.6 1.3 copy-start.2
  99.7 1.3 copy-start.3
  101.0 22.8 %copy-start.4 = (s32[32]{0:T(128)S(1)}, s32[32]{0:T(128)}, u32[]{:S(2)}) copy-start(s32[32]{0:T(128)} %broadcast_xor_fusion.ids_ref) | copy-start | bytes 388
  183.1 33.2 %all-to-all-start = ((f32[32,3,2048]{2,1,0:T(4,128)}), f32[32,3,2048]{2,1,0:T(4,128)S(1)}, u32[]{:S(2)}, u32[]{:S(2)}) async-start(f32[32,3,2048]{2,1,0:T(4,128)} %interpolate.1), calls=%async_computation | async-start | bytes 2097152 | tf_op jit(solution)/shard_map/all_to_all | solution.py:489
